TPU v7x, 32 devices: a whole 2x2x4 slice. The times are simulated.
32 devices in a mesh: blk: 8 (over y, x, core), head: 4 (over z).
Axes of the slice: x: 2, y: 2, z: 4, core: 2. Of those that a mesh axis runs over, the one named last changes fastest.
Arguments:
- tokens: bfloat16 [8, 1024, 768], P(None, ('blk', 'head')), may hold values from -6 to 6
- chain_id: int32 [1024], P(('blk', 'head')), may hold values from 0 to 3, never falling along the last dimension, each value on 1 to 512 neighbouring positions
- hotspots: int32 [16], replicated, may hold values from 0 to 1023
- chain_embed: bfloat16 [4, 768], replicated, may hold values from -6 to 6
- hot_embed: bfloat16 [768], replicated, may hold values from -6 to 6
- w_proj: bfloat16 [768, 3072], P(None, 'head'), may hold values from -0.21875 to 0.21875
- pair_bias: bfloat16 [16, 1024, 1024], P('head', 'blk'), may hold values from -400 to 400
- w_out: bfloat16 [768, 768], P('head'), may hold values from -0.21875 to 0.21875
Outputs:
- update: bfloat16 [8, 1024, 768], P(None, ('blk', 'head'))
Inputs may be any that keep to these rules, and one draw needn't show every extreme that they name: `chain_id`: chain ids never fall along the tokens; one chain has exactly 512 tokens. `hotspots`: positions may repeat.
All inputs are finite; a program needn't handle non-finite values.
Results may differ from a plain program's by a relative error of at most 0.02.
Values may be sent and summed in bfloat16 or wider, within the bound.
A program may use at most 64 MiB of HBM per device.

v0:
```python
import jax
import jax.numpy as jnp
from jax import lax
from jax.sharding import PartitionSpec as P

HD = 48


def attend_keys(state, queries, key_blk, value_blk, bias_blk):
    row_max, row_sum, weighted = state
    scores = jnp.einsum("sqhd,shdk->shqk", queries, key_blk, preferred_element_type=jnp.float32)
    scores = scores + bias_blk.astype(jnp.float32)[None]
    new_max = jnp.maximum(row_max, jnp.max(scores, axis=-1))
    rescale = jnp.exp(row_max - new_max)
    probs = jnp.exp(scores - new_max[..., None])
    row_sum = row_sum * rescale + jnp.sum(probs, axis=-1)
    partial_out = jnp.einsum(
        "shqk,shdk->shqd", probs.astype(jnp.bfloat16), value_blk, preferred_element_type=jnp.float32
    )
    weighted = weighted * rescale[..., None] + partial_out
    return (new_max, row_sum, weighted)


def body(tokens, chain_id, hotspots, chain_embed, hot_embed, w_proj, pair_bias, w_out):
    samples, tok_dev, width = tokens.shape
    groups = lax.axis_size("head")
    first_tok = (lax.axis_index("blk") * groups + lax.axis_index("head")) * tok_dev
    positions = first_tok + jnp.arange(tok_dev, dtype=jnp.int32)
    is_hot = jnp.any(positions[:, None] == hotspots[None, :], axis=1).astype(jnp.float32)
    onehot = (
        chain_id[:, None] == jnp.arange(chain_embed.shape[0], dtype=jnp.int32)[None, :]
    ).astype(jnp.float32)
    condition = jnp.sum(onehot[:, :, None] * chain_embed.astype(jnp.float32)[None], axis=1)
    condition = condition + is_hot[:, None] * hot_embed.astype(jnp.float32)[None, :]
    shifted = tokens.astype(jnp.float32) + condition[None]
    average = jnp.mean(shifted, axis=-1, keepdims=True)
    spread = jnp.mean((shifted - average) ** 2, axis=-1, keepdims=True)
    normed = ((shifted - average) * lax.rsqrt(spread + 1e-05)).astype(jnp.bfloat16)
    block_tokens = lax.all_gather(normed, "head", axis=1, tiled=True)
    tok_blk = block_tokens.shape[1]
    heads_here = w_proj.shape[1] // (4 * HD)
    proj = jnp.dot(
        block_tokens.reshape(samples * tok_blk, width), w_proj, preferred_element_type=jnp.float32
    )
    proj = proj.reshape(samples, tok_blk, heads_here, 4, HD)
    queries = (proj[:, :, :, 0] * (1.0 / HD**0.5)).astype(jnp.bfloat16)
    keys_t = jnp.transpose(proj[:, :, :, 1], (0, 2, 3, 1)).astype(jnp.bfloat16)
    values_t = jnp.transpose(proj[:, :, :, 2], (0, 2, 3, 1)).astype(jnp.bfloat16)
    gating = jax.nn.sigmoid(proj[:, :, :, 3])
    start_state = (
        jnp.full((samples, heads_here, tok_blk), -jnp.inf, jnp.float32),
        jnp.zeros((samples, heads_here, tok_blk), jnp.float32),
        jnp.zeros((samples, heads_here, tok_blk, HD), jnp.float32),
    )
    key_part = lax.all_gather(keys_t, "blk", axis=3, tiled=True)
    value_part = lax.all_gather(values_t, "blk", axis=3, tiled=True)
    key_rows = key_part.shape[3]
    block_size = 512
    count = key_rows // block_size
    key_blocks = jnp.moveaxis(key_part.reshape(samples, heads_here, HD, count, block_size), 3, 0)
    value_blocks = jnp.moveaxis(
        value_part.reshape(samples, heads_here, HD, count, block_size), 3, 0
    )
    bias_blocks = jnp.moveaxis(pair_bias.reshape(heads_here, tok_blk, count, block_size), 2, 0)

    def scan_body(inner, blocks_in):
        return (attend_keys(inner, queries, blocks_in[0], blocks_in[1], blocks_in[2]), None)

    final, unused = lax.scan(scan_body, start_state, (key_blocks, value_blocks, bias_blocks))
    row_max, row_sum, weighted = final
    attended = jnp.transpose(weighted / row_sum[..., None], (0, 2, 1, 3))
    gated = (attended * gating).astype(jnp.bfloat16).reshape(samples, tok_blk, heads_here * HD)
    summed = lax.psum_scatter(
        jnp.einsum("std,de->tse", gated, w_out, preferred_element_type=jnp.float32).astype(
            jnp.bfloat16
        ),
        "head",
        scatter_dimension=0,
        tiled=True,
    ).astype(jnp.float32)
    update = jnp.transpose(summed, (1, 0, 2))
    return update.astype(jnp.bfloat16)


def solution(mesh):
    in_specs = (
        P(None, ("blk", "head"), None),
        P(("blk", "head")),
        P(),
        P(),
        P(),
        P(None, "head"),
        P("head", "blk", None),
        P("head", None),
    )
    out_specs = P(None, ("blk", "head"), None)
    return jax.shard_map(body, mesh=mesh, in_specs=in_specs, out_specs=out_specs, check_vma=False)
```

profile of v0, /device:TPU:0, one launch (start us, length us, event | category | flops | bytes accessed | tf_op | source)
XLA Modules:
  0.0 207.8 jit_solution(2871459851759996685)
XLA Ops:
  9.6 1.1 fusion.30
  10.8 1.2 multiply_reduce_fusion
  12.0 1.9 multiply_convert_fusion
  14.7 39.2 %all-gather.4.cloned.1.call-done = bf16[8,128,768]{2,1,0:T(8,128)(2,1)} async-done(((bf16[8,32,768]{2,1,0:T(8,128)(2,1)}), bf16[8,128,768]{2,1,0:T(8,128)(2,1)}) %all-gather.4.cloned.1.call-update) | async-done | bytes 1572880 | tf_op jit(solution)/shard_map/all_gather | solution.py:39
  53.9 4.6 %fusion.35 = (bf16[8,128,4,4,48]{1,4,3,2,0:T(8,128)(2,1)S(1)}, f32[8,128,4,4,48]{1,4,3,2,0:T(8,128)}) fusion(bf16[4,4,48,768,1]{3,2,1,0,4:T(8,128)(2,1)S(1)} %bitcast.107, bf16[8,128,768]{2,1,0:T(8,128)(2,1)} %all-gather.4.cloned.1.call-done), kind=kOutput, calls=%fused_computation.54 | convolution fusion | flops 1208745984 | bytes 7471104 | tf_op jit(solution)/shard_map/dot_general | solution.py:42
  58.5 1.0 slice_bitcast_fusion
  60.4 2.3 %copy.22 = bf16[4,128,1024]{1,2,0:T(8,128)(2,1)} copy(bf16[4,128,1024]{2,1,0:T(8,128)(2,1)} %param.16) | data formatting | bytes 2097152 | tf_op args[6]
  62.7 1.2 fusion.32
  63.9 27.5 %all-gather.8.cloned.1.call-done = bf16[8,4,48,1024]{3,2,1,0:T(8,128)(2,1)} async-done(((bf16[8,4,48,128]{3,2,1,0:T(8,128)(2,1)}), bf16[8,4,48,1024]{3,2,1,0:T(8,128)(2,1)}) %all-gather.8.cloned.1.call-update) | async-done | bytes 3145744 | tf_op jit(solution)/shard_map/all_gather | solution.py:56
  91.4 4.1 %copy.32 = bf16[8,4,6,2,8,512]{5,4,2,1,0,3:T(8,128)(2,1)} copy(bf16[8,4,6,2,8,512]{5,4,3,2,1,0:T(8,128)(2,1)} %bitcast.104) | data formatting | bytes 6291456 | tf_op jit(solution)/shard_map/reshape | solution.py:62
  95.5 30.6 %all-gather.6.cloned.1.call-done = bf16[8,4,48,1024]{3,2,1,0:T(8,128)(2,1)} async-done(((bf16[8,4,48,128]{3,2,1,0:T(8,128)(2,1)}), bf16[8,4,48,1024]{3,2,1,0:T(8,128)(2,1)}) %all-gather.6.cloned.1.call-update) | async-done | bytes 3145744 | tf_op jit(solution)/shard_map/all_gather | solution.py:55
  126.1 4.0 %copy.33 = bf16[8,4,6,2,8,512]{5,4,2,1,0,3:T(8,128)(2,1)} copy(bf16[8,4,6,2,8,512]{5,4,3,2,1,0:T(8,128)(2,1)} %bitcast.105) | data formatting | bytes 6291456 | tf_op jit(solution)/shard_map/reshape | solution.py:60
  130.1 32.5 %while.15 = (s32[]{:T(128)}, f32[8,4,128]{2,1,0:T(4,128)S(1)}, f32[8,4,128]{2,1,0:T(4,128)S(1)}, f32[8,4,128,48]{2,3,1,0:T(8,128)S(1)}, bf16[2,8,4,48,512]{4,3,2...) while((s32[]{:T(128)}, f32[8,4,128]{2,1,0:T(4,128)S(1)}, ...), condition=%wide.region_7.8_spmd.clone, body=%wide.region_4.7_spmd.clone.sunk | while | flops 420302848 | bytes 68813968 | solution.py:69
  130.1 1.1 bitcast_convert_fusion.2
  131.2 6.1 %fusion.49 = (f32[8,4,128]{2,1,0:T(4,128)S(1)}, f32[8,4,512,128]{3,2,1,0:T(8,128)}) fusion(f32[4,128,512]{1,2,0:T(8,128)S(1)} %bitcast_convert_fusion.2, bf16[8,128,4,48]{1,3,2,0:T(8,128)(2,1)S(1)} %get-tuple-element.199, bf16[2,8,4,48,512]{4,3,2,1,0:T(8,128)(2,1)} %get-tuple-element.198, s32[]{:T(128)} %get-tuple-element.184), kind=kOutput, calls=%fused_computation.2.clone.1 | convolution fusion | flops 205516800 | bytes 11420160 | tf_op jit(solution)/shard_map/while/body/eval_jaxpr/sqhd,shdk->shqk/dot_general | solution.py:11
  137.3 5.0 %fusion.50 = f32[8,4,128]{2,1,0:T(4,128)S(1)} fusion(f32[8,4,512,128]{3,2,1,0:T(8,128)} %get-tuple-element.171, f32[8,4,128]{2,1,0:T(4,128)S(1)} %select_maximum_fusion.2, f32[4,128,512]{1,2,0:T(8,128)S(1)} %bitcast_convert_fusion.2), kind=kLoop, calls=%fused_computation.4.clone.1 | loop fusion | flops 6287360 | bytes 9469952 | tf_op jit(solution)/shard_map/while/body/eval_jaxpr/reduce_sum | solution.py:16
  143.1 3.3 %fusion.52 = f32[8,4,128,48]{2,3,1,0:T(8,128)S(1)} fusion(f32[8,4,512,128]{3,2,1,0:T(8,128)S(1)} %copy-done.1, f32[8,4,128]{2,1,0:T(4,128)S(1)} %select_maximum_fusion.2, f32[4,128,512]{1,2,0:T(8,128)S(1)} %bitcast_convert_fusion.2, bf16[2,8,4,48,512]{4,3,2,1,0:T(8,128)(2,1)} %get-tuple-element.201, s32[]{:T(128)} %get-tuple-element.184, ...), kind=kOutput, calls=%fused_computation.13.clone.1 | convolution fusion | flops 208207872 | bytes 12616193 | tf_op jit(solution)/shard_map/while/body/eval_jaxpr/shqk,shdk->shqd/dot_general | solution.py:17
  146.4 1.1 bitcast_convert_fusion.2
  147.5 6.1 %fusion.49 = (f32[8,4,128]{2,1,0:T(4,128)S(1)}, f32[8,4,512,128]{3,2,1,0:T(8,128)}) fusion(f32[4,128,512]{1,2,0:T(8,128)S(1)} %bitcast_convert_fusion.2, bf16[8,128,4,48]{1,3,2,0:T(8,128)(2,1)S(1)} %get-tuple-element.199, bf16[2,8,4,48,512]{4,3,2,1,0:T(8,128)(2,1)} %get-tuple-element.198, s32[]{:T(128)} %get-tuple-element.184), kind=kOutput, calls=%fused_computation.2.clone.1 | convolution fusion | flops 205516800 | bytes 11420160 | tf_op jit(solution)/shard_map/while/body/eval_jaxpr/sqhd,shdk->shqk/dot_general | solution.py:11
  153.6 5.0 %fusion.50 = f32[8,4,128]{2,1,0:T(4,128)S(1)} fusion(f32[8,4,512,128]{3,2,1,0:T(8,128)} %get-tuple-element.171, f32[8,4,128]{2,1,0:T(4,128)S(1)} %select_maximum_fusion.2, f32[4,128,512]{1,2,0:T(8,128)S(1)} %bitcast_convert_fusion.2), kind=kLoop, calls=%fused_computation.4.clone.1 | loop fusion | flops 6287360 | bytes 9469952 | tf_op jit(solution)/shard_map/while/body/eval_jaxpr/reduce_sum | solution.py:16
  159.3 3.3 %fusion.52 = f32[8,4,128,48]{2,3,1,0:T(8,128)S(1)} fusion(f32[8,4,512,128]{3,2,1,0:T(8,128)S(1)} %copy-done.1, f32[8,4,128]{2,1,0:T(4,128)S(1)} %select_maximum_fusion.2, f32[4,128,512]{1,2,0:T(8,128)S(1)} %bitcast_convert_fusion.2, bf16[2,8,4,48,512]{4,3,2,1,0:T(8,128)(2,1)} %get-tuple-element.201, s32[]{:T(128)} %get-tuple-element.184, ...), kind=kOutput, calls=%fused_computation.13.clone.1 | convolution fusion | flops 208207872 | bytes 12616193 | tf_op jit(solution)/shard_map/while/body/eval_jaxpr/shqk,shdk->shqd/dot_general | solution.py:17
  162.7 1.4 fusion.31
  164.0 1.8 fusion.22
  165.8 35.4 %reduce-scatter.2.cloned.1.call-done = bf16[32,8,768]{2,0,1:T(8,128)(2,1)} async-done(((bf16[128,8,768]{2,0,1:T(8,128)(2,1)}), bf16[32,8,768]{2,0,1:T(8,128)(2,1)}) %reduce-scatter.2.cloned.1.call-update) | async-done | bytes 393232 | tf_op jit(solution)/shard_map/reduce_scatter | solution.py:73
  (36 shorter events, 6.1 us)
Async XLA Ops:
  6.5 157.5 %copy-start = (bf16[192,768]{1,0:T(8,128)(2,1)S(1)}, bf16[192,768]{1,0:T(8,128)(2,1)}, u32[]{:S(2)}) copy-start(bf16[192,768]{1,0:T(8,128)(2,1)} %param.17) | copy-start | bytes 884740
  6.5 7.5 %copy-start.2 = (bf16[768,768]{1,0:T(8,128)(2,1)S(1)}, bf16[768,768]{1,0:T(8,128)(2,1)}, u32[]{:S(2)}) copy-start(bf16[768,768]{1,0:T(8,128)(2,1)} %param.15) | copy-start | bytes 3538948
  6.5 47.4 %all-gather.4.cloned.1.call-start = ((), (), s32[]{:S(2)}) async-start(), calls=%async_computation.1 | async-start | bytes 1966080 | tf_op jit(solution)/shard_map/all_gather | solution.py:39
  14.0 77.4 %all-gather.8.cloned.1.call-start = ((), (), s32[]{:S(2)}) async-start(), calls=%async_computation.3 | async-start | bytes 3538944 | tf_op jit(solution)/shard_map/all_gather | solution.py:56
  59.5 66.6 %all-gather.6.cloned.1.call-start = ((), (), s32[]{:S(2)}) async-start(), calls=%async_computation.2 | async-start | bytes 3538944 | tf_op jit(solution)/shard_map/all_gather | solution.py:55
  60.3 141.0 %reduce-scatter.2.cloned.1.call-start = ((), (), s32[]{:S(2)}) async-start(), calls=%async_computation.4 | async-start | bytes 1966080 | tf_op jit(solution)/shard_map/reduce_scatter | solution.py:73
  137.3 5.8 %copy-start.1 = (f32[8,4,512,128]{3,2,1,0:T(8,128)S(1)}, f32[8,4,512,128]{3,2,1,0:T(8,128)}, u32[]{:S(2)}) copy-start(f32[8,4,512,128]{3,2,1,0:T(8,128)} %get-tuple-element.171) | copy-start | bytes 25165828 | tf_op jit(solution)/shard_map/while
  153.6 5.8 %copy-start.1 = (f32[8,4,512,128]{3,2,1,0:T(8,128)S(1)}, f32[8,4,512,128]{3,2,1,0:T(8,128)}, u32[]{:S(2)}) copy-start(f32[8,4,512,128]{3,2,1,0:T(8,128)} %get-tuple-element.171) | copy-start | bytes 25165828 | tf_op jit(solution)/shard_map/while
Sparse Core Ops, SparseCore 0:
  14.1 39.7 all-gather.3
  59.7 31.6 all-gather.7
  93.3 32.8 all-gather.5
  166.0 35.2 reduce-scatter.1
where the time goes:
time: 209 us; the launch traced here: 208 us
  waiting for transfers between devices  134 us (64%)
  matrix products  25.1 us (12%)
  other arithmetic  22.3 us (11%)
  local copies, waits for them, and re-layouts  13.4 us (6%)
  between operations  13.2 us (6%)
    all_gather x1, waiting for transfers between devices, body(): block_tokens = lax.all_gather(normed, 'head', axis=1, tiled=True)  39.2 us
    reduce_scatter x1, waiting for transfers between devices, body(): lax.psum_scatter(jnp.einsum('std,de->tse', gated, w_out, preferred_elemen...  35.4 us
    all_gather x1, waiting for transfers between devices, body(): key_part = lax.all_gather(keys_t, 'blk', axis=3, tiled=True)  30.6 us
    all_gather x1, waiting for transfers between devices, body(): value_part = lax.all_gather(values_t, 'blk', axis=3, tiled=True)  27.5 us
    dot_general x2, matrix products, attend_keys(): jnp.einsum('sqhd,shdk->shqk', queries, key_blk, preferred_element_type=jn...  12.1 us
    reduce_sum x2, other arithmetic, attend_keys(): row_sum = row_sum * rescale + jnp.sum(probs, axis=-1)  10 us
    dot_general x2, matrix products, attend_keys(): jnp.einsum('shqk,shdk->shqd', probs.astype(jnp.bfloat16), value_blk, pref...  6.57 us
    dot_general x1, matrix products, body(): jnp.dot(block_tokens.reshape(samples * tok_blk, width), w_proj, preferred...  4.61 us
  transfers between devices with their start and end apart: 4, of which 4 were waited for; matrix products, arithmetic and copies ran while one was open for 4% of the time, Pallas kernels for 0%

commit v1 on v0

v1 whole, which is shorter than its diff:
```python
import functools
import jax
import jax.numpy as jnp
from jax import lax
from jax.experimental import pallas as pl
from jax.experimental.pallas import tpu as pltpu
from jax.sharding import PartitionSpec as P

HD = 48
MESH = pl.DeviceIdType.MESH


def flip(index, bits, count):
    total = 0
    weight = 1
    while weight < count:
        bit = (index // weight) % 2
        total = total + ((1 - bit) if (bits // weight) % 2 else bit) * weight
        weight *= 2
    return total


def low_bit(r):
    return r & -r


def high_bit(r):
    return 1 << (r.bit_length() - 1)


def kernel(
    n, nb, chain_ref, hot_ref, tok_ref, cemb_ref, hemb_ref, w_ref, bias_ref, wout_ref, out_ref,
    x_all, table, cond, w_t, kv, q_all, gate_all, gout, gin, wo,
    xs_sem, xr_sem, ws_sem, wr_sem, ks_sem, kr_sem, gs_sem, gr_sem,
):
    samples, td, width = tok_ref.shape
    hh = bias_ref.shape[0]
    tb = n * td
    cols = hh * HD
    z = lax.axis_index("head")
    b = lax.axis_index("blk")
    bits = [1 << k for k in range(nb.bit_length() - 1)]

    barrier = pltpu.get_barrier_semaphore()
    for o in range(1, n):
        pl.semaphore_signal(
            barrier, inc=1, device_id={"blk": b, "head": (z + o) % n}, device_id_type=MESH
        )
    for bit in bits:
        pl.semaphore_signal(
            barrier, inc=1, device_id={"blk": flip(b, bit, nb), "head": z}, device_id_type=MESH
        )

    def line_copy(at, send, recv, block, to):
        return pltpu.make_async_remote_copy(
            src_ref=at(block), dst_ref=at(block), send_sem=send, recv_sem=recv,
            device_id={"blk": b, "head": to}, device_id_type=MESH,
        )

    def line_send(at, send, recv, d, act):
        @pl.when((z - d + 1 >= 0) & (z + 1 < n))
        def _():
            act(line_copy(at, send(0, d), recv(0, d), z - d + 1, z + 1))

        @pl.when((z + d - 1 < n) & (z >= 1))
        def _():
            act(line_copy(at, send(1, d), recv(1, d), z + d - 1, z - 1))

    def line_recv(at, send, recv, d):
        @pl.when(z - d >= 0)
        def _():
            line_copy(at, send(0, d), recv(0, d), z - d, z - 1).wait_recv()

        @pl.when(z + d < n)
        def _():
            line_copy(at, send(1, d), recv(1, d), z + d, z + 1).wait_recv()

    def x_line(s):
        return (
            lambda j: x_all.at[s, j],
            lambda way, d: xs_sem.at[s, way, d - 1],
            lambda way, d: xr_sem.at[s, way, d - 1],
        )

    w_line = (
        lambda j: wo.at[j],
        lambda way, d: ws_sem.at[way, d - 1],
        lambda way, d: wr_sem.at[way, d - 1],
    )

    def route(s, r):
        if r % 2:
            return flip(b, r - 1, nb), flip(b, 1, nb), flip(b, r, nb)
        first, second = low_bit(r), high_bit(r)
        odd = s % 2
        blocks = [flip(b, r ^ step, nb) for step in (second, first)]
        peers = [flip(b, step, nb) for step in (second, first)]
        return (
            blocks[0] * (1 - odd) + blocks[1] * odd,
            peers[0] * (1 - odd) + peers[1] * odd,
            flip(b, r, nb),
        )

    def kv_send(s, r):
        block, peer, _ = route(s, r)
        return pltpu.make_async_remote_copy(
            src_ref=kv.at[s, block], dst_ref=kv.at[s, block],
            send_sem=ks_sem.at[s, r], recv_sem=kr_sem.at[s, r],
            device_id={"blk": peer, "head": z}, device_id_type=MESH,
        )

    def kv_recv(s, r):
        _, peer, mine = route(s, r)
        pltpu.make_async_remote_copy(
            src_ref=kv.at[s, mine], dst_ref=kv.at[s, mine],
            send_sem=ks_sem.at[s, r], recv_sem=kr_sem.at[s, r],
            device_id={"blk": peer, "head": z}, device_id_type=MESH,
        ).wait_recv()

    def gated_copy(s, o):
        to = (z + o) % n
        return pltpu.make_async_remote_copy(
            src_ref=gout.at[s, to], dst_ref=gin.at[s, z],
            send_sem=gs_sem.at[s, o], recv_sem=gr_sem.at[s, o],
            device_id={"blk": b, "head": to}, device_id_type=MESH,
        )

    def gated_recv(s, o):
        source = (z + n - o) % n
        pltpu.make_async_remote_copy(
            src_ref=gin.at[s, source], dst_ref=gin.at[s, source],
            send_sem=gs_sem.at[s, o], recv_sem=gr_sem.at[s, o],
            device_id={"blk": b, "head": source}, device_id_type=MESH,
        ).wait_recv()

    rows = lax.broadcasted_iota(jnp.int32, (td, 128), 0)
    lanes = lax.broadcasted_iota(jnp.int32, (td, 128), 1)
    chains = cemb_ref.shape[0]
    chain = jnp.zeros((td, 128), jnp.int32)
    for i in range(td):
        chain = jnp.where(rows == i, chain_ref[i], chain)
    position = (b * n + z) * td + rows
    hot = jnp.zeros((td, 128), jnp.int32)
    for i in range(hot_ref.shape[0]):
        hot = jnp.where(position == hot_ref[i], 1, hot)
    picks = jnp.where(lanes == chain, 1.0, jnp.where(lanes == chains, hot.astype(jnp.float32), 0.0))
    table[...] = jnp.zeros_like(table)
    table[0:chains] = cemb_ref[...].astype(jnp.float32)
    table[chains : chains + 1] = hemb_ref[...].astype(jnp.float32)
    cond[...] = jnp.dot(
        picks.astype(jnp.bfloat16), table[...].astype(jnp.bfloat16), preferred_element_type=jnp.float32
    )

    pl.semaphore_wait(barrier, n - 1 + len(bits))

    def normalize(s, carry):
        shifted = tok_ref[s].astype(jnp.float32) + cond[...]
        average = jnp.mean(shifted, axis=-1, keepdims=True)
        centered = shifted - average
        spread = jnp.mean(centered * centered, axis=-1, keepdims=True)
        x_all[s, z] = (centered * lax.rsqrt(spread + 1e-05)).astype(jnp.bfloat16)
        line_send(*x_line(s), 1, lambda copy: copy.start())
        return carry

    lax.fori_loop(0, samples, normalize, 0)

    wo[z] = wout_ref[...]
    tile = 128 if w_ref.shape[1] % 128 == 0 else w_ref.shape[1]
    for c in range(0, w_ref.shape[1], tile):
        w_t[c : c + tile] = w_ref[:, c : c + tile].astype(jnp.float32).T.astype(jnp.bfloat16)

    evens = [r for r in range(2, nb, 2)]
    levels = max(bin(r).count("1") for r in evens)
    attend_lag = levels + 1
    out_lag = attend_lag + 1

    def at_sample(s, act):
        @pl.when((s >= 0) & (s < samples))
        def _():
            act(s)

    def project(s):
        x = x_all[s].reshape(tb, width)
        proj = lax.dot_general(
            w_t[...], x, (((1,), (1,)), ((), ())), preferred_element_type=jnp.float32
        )
        keys, values = [], []
        for h in range(hh):
            base = h * 4 * HD
            keys.append(proj[base + HD : base + 2 * HD])
            values.append(proj[base + 2 * HD : base + 3 * HD])
        kv[s, b] = jnp.concatenate(keys + values, axis=0).astype(jnp.bfloat16)
        for bit in bits:
            kv_send(s, bit).start()
        for h in range(hh):
            base = h * 4 * HD
            q_all[s, h] = (proj[base : base + HD] * (1.0 / HD**0.5)).T.astype(jnp.bfloat16)
            gate_all[s, h] = jax.nn.sigmoid(proj[base + 3 * HD : base + 4 * HD]).T

    def forward(level):
        def act(s):
            for r in evens:
                if bin(r).count("1") != level:
                    continue
                kv_recv(s, r)
                kv_send(s, r + 1).start()
                for bit in bits[1:]:
                    if r & bit:
                        continue
                    later = r | bit
                    first, second = low_bit(later), high_bit(later)
                    if bit == second:

                        @pl.when(s % 2 == 0)
                        def _(later=later):
                            kv_send(s, later).start()

                    if bit == first:

                        @pl.when(s % 2 == 1)
                        def _(later=later):
                            kv_send(s, later).start()

        return act

    def attend(s):
        for r in range(1, nb, 2):
            kv_recv(s, r)
        ones = jnp.ones((16, nb * tb), jnp.bfloat16)
        parts = []
        for h in range(hh):
            key = jnp.concatenate([kv[s, a, h * HD : (h + 1) * HD, :] for a in range(nb)], axis=1)
            value = jnp.concatenate(
                [kv[s, a, cols + h * HD : cols + (h + 1) * HD, :] for a in range(nb)], axis=1
            )
            scores = jnp.dot(q_all[s, h], key, preferred_element_type=jnp.float32)
            scores = scores + bias_ref[h].astype(jnp.float32)
            top = jnp.max(scores, axis=-1, keepdims=True)
            probs = jnp.exp(scores - top).astype(jnp.bfloat16)
            weighted = lax.dot_general(
                probs, jnp.concatenate([value, ones], axis=0), (((1,), (1,)), ((), ())),
                preferred_element_type=jnp.float32,
            )
            parts.append(weighted[:, :HD] / weighted[:, HD : HD + 1] * gate_all[s, h])
        gated = jnp.concatenate(parts, axis=1)
        for j in range(n):
            gout[s, j] = gated[j * td : (j + 1) * td].astype(jnp.bfloat16)
        for o in range(1, n):
            gated_copy(s, o).start()
        gin[s, z] = gout[s, z]

    def project_out(s):
        for o in range(1, n):
            gated_recv(s, o)
        total = jnp.zeros((td, width), jnp.float32)
        for j in range(n):
            total = total + jnp.dot(gin[s, j], wo[j], preferred_element_type=jnp.float32)
        out_ref[s] = total.astype(out_ref.dtype)

    def step(t, carry):
        for d in range(1, n):

            def hop(s, d=d):
                line_recv(*x_line(s), d)
                if d + 1 < n:
                    line_send(*x_line(s), d + 1, lambda copy: copy.start())

            at_sample(t + (n - 1 - d), hop)
        for level in range(1, levels + 1):
            at_sample(t - level, forward(level))
        at_sample(t, project)

        @pl.when(t == 0)
        def _():
            line_send(*w_line, 1, lambda copy: copy.start())

        for d in range(1, n):

            @pl.when(t == min(d + 1, out_lag))
            def _(d=d):
                line_recv(*w_line, d)
                if d + 1 < n:
                    line_send(*w_line, d + 1, lambda copy: copy.start())

        at_sample(t - attend_lag, attend)
        at_sample(t - out_lag, project_out)
        return carry

    lax.fori_loop(-(n - 2), samples + out_lag, step, 0)

    def drain(s, carry):
        for d in range(1, n):
            line_send(*x_line(s), d, lambda copy: copy.wait_send())
        for r in range(1, nb):
            kv_send(s, r).wait_send()
        for o in range(1, n):
            gated_copy(s, o).wait_send()
        return carry

    lax.fori_loop(0, samples, drain, 0)
    for d in range(1, n):
        line_send(*w_line, d, lambda copy: copy.wait_send())


def body(n, nb, tokens, chain_id, hotspots, chain_embed, hot_embed, w_proj, pair_bias, w_out):
    samples, td, width = tokens.shape
    hh, tb, keys = pair_bias.shape
    cols = hh * HD
    smem = pl.BlockSpec(memory_space=pltpu.SMEM)
    vmem = pl.BlockSpec(memory_space=pltpu.VMEM)
    bf16, f32 = jnp.bfloat16, jnp.float32
    dma = pltpu.SemaphoreType.DMA
    return pl.pallas_call(
        functools.partial(kernel, n, nb),
        out_shape=jax.ShapeDtypeStruct((samples, td, width), bf16),
        in_specs=[smem, smem] + [vmem] * 6,
        out_specs=vmem,
        scratch_shapes=[
            pltpu.VMEM((samples, n, td, width), bf16),
            pltpu.VMEM((128, width), f32),
            pltpu.VMEM((td, width), f32),
            pltpu.VMEM((w_proj.shape[1], width), bf16),
            pltpu.VMEM((samples, nb, 2 * cols, tb), bf16),
            pltpu.VMEM((samples, hh, tb, HD), bf16),
            pltpu.VMEM((samples, hh, tb, HD), f32),
            pltpu.VMEM((samples, n, td, cols), bf16),
            pltpu.VMEM((samples, n, td, cols), bf16),
            pltpu.VMEM((n, cols, width), bf16),
            dma((samples, 2, n - 1)),
            dma((samples, 2, n - 1)),
            dma((2, n - 1)),
            dma((2, n - 1)),
            dma((samples, nb)),
            dma((samples, nb)),
            dma((samples, n)),
            dma((samples, n)),
        ],
        compiler_params=pltpu.CompilerParams(
            collective_id=0, has_side_effects=True, vmem_limit_bytes=56 * 1024 * 1024
        ),
    )(chain_id, hotspots, tokens, chain_embed, hot_embed.reshape(1, width), w_proj, pair_bias, w_out)


def solution(mesh):
    in_specs = (
        P(None, ("blk", "head"), None),
        P(("blk", "head")),
        P(),
        P(),
        P(),
        P(None, "head"),
        P("head", "blk", None),
        P("head", None),
    )
    out_specs = P(None, ("blk", "head"), None)
    run = functools.partial(body, mesh.shape["head"], mesh.shape["blk"])
    return jax.shard_map(run, mesh=mesh, in_specs=in_specs, out_specs=out_specs, check_vma=False)
```

time: 209 us -> 87.1 us (0.42)
  waiting for transfers between devices: 134 us -> 0 us
  Pallas kernels: 0 us -> 83.8 us
  matrix products: 25.1 us -> 0 us
  other arithmetic: 22.3 us -> 0 us
  between operations: 13.2 us -> 0.01 us
  local copies, waits for them, and re-layouts: 13.4 us -> 3.03 us
    all_gather x3 -> x0, waiting for transfers between devices: 97.4 us -> none  [the longest x1 39.2 us: body(): block_tokens = lax.all_gather(normed, 'head', axis=1, tiled=True)]
    pallas_call x0 -> x1, Pallas kernels: none -> 83.8 us  [body(): pl.pallas_call(functools.partial(kernel, n, nb), out_shape=jax.ShapeDtype...]
    reduce_scatter x1 -> x0, waiting for transfers between devices: 35.4 us -> none  [body(): lax.psum_scatter(jnp.einsum('std,de->tse', gated, w_out, preferred_elemen...]
    dot_general x6 -> x0, matrix products: 25.1 us -> none  [the longest x2 12.1 us: attend_keys(): jnp.einsum('sqhd,shdk->shqk', queries, key_blk, preferred_element_type=jn...]
    reduce_sum x5 -> x0, other arithmetic: 12.5 us -> none  [the longest x2 10 us: attend_keys(): row_sum = row_sum * rescale + jnp.sum(probs, axis=-1)]
    reshape x2 -> x1, local copies, waits for them, and re-layouts: 8.09 us -> 1.26 us  [body(): hot_embed.reshape(1, width)]
    convert_element_type x7 -> x0, other arithmetic: 6.55 us -> none  [the longest x1 1.91 us: body(): ((shifted - average) * lax.rsqrt(spread + 1e-05)).astype(jnp.bfloat16)]
    add x6 -> x0, other arithmetic: 2.37 us -> none  [the longest x2 2.23 us: attend_keys(): scores = scores + bias_blk.astype(jnp.float32)[None]]
  transfers between devices with their start and end apart: 4 -> 0, of which waited for: 4 -> 0; matrix products, arithmetic and copies ran while one was open for 4% -> 0% of each run, Pallas kernels for 0% -> 0%
where the time goes in v1:
time: 87.1 us; the launch traced here: 86.9 us
  Pallas kernels  83.8 us (96%)
  local copies, waits for them, and re-layouts  3.03 us (3%)
    pallas_call x1, Pallas kernels, body(): pl.pallas_call(functools.partial(kernel, n, nb), out_shape=jax.ShapeDtype...  83.8 us
    unnamed x1, local copies, waits for them, and re-layouts  1.77 us

profile of v1, /device:TPU:0, one launch (start us, length us, event | category | flops | bytes accessed | tf_op | source)
XLA Modules:
  0.0 86.9 jit_solution(8897843734905371616)
XLA Ops:
  0.0 1.3 %reshape.3.hemb_ref = bf16[1,768]{1,0:T(2,128)(2,1)} reshape(bf16[768]{0:T(1024)(128)(2,1)} %param.12) | data formatting | bytes 3072 | tf_op jit(solution)/shard_map/reshape | solution.py:341
  1.3 83.8 %shard_map.82 = bf16[8,32,768]{2,1,0:T(8,128)(2,1)} custom-call(s32[32]{0:T(128)} %chain_ref.1, s32[16]{0:T(128)} %hot_ref.1, bf16[8,32,768]{2,1,0:T(8,128)(2,1)} %tok_ref.1, bf16[4,768]{1,0:T(4,128)(2,1)} %cemb_ref.1, bf16[1,768]{1,0:T(2,128)(2,1)} %reshape.3.hemb_ref, bf16[768,768]{1,0:T(8,128)(2,1)} %w_ref.1, bf16[4,128,1024]{2,1,0:T(8,128)(2,1)} %bias_ref.1, ...), custom_call_target="tpu_custom_call" | custom-call | tf_op jit(solution)/shard_map/pallas_call | solution.py:313
  85.1 1.8 %copy.10 = bf16[8,32,768]{2,1,0:T(8,128)(2,1)} copy(bf16[8,32,768]{2,1,0:T(8,128)(2,1)} %shard_map.82) | data formatting | bytes 786432

commit v2 on v1

--- a/solution.py
+++ b/solution.py
@@ -7,6 +7,7 @@
 from jax.sharding import PartitionSpec as P
 
 HD = 48
+LOG2E = 1.4426950408889634
 MESH = pl.DeviceIdType.MESH
 
 
@@ -30,7 +31,7 @@
 
 def kernel(
     n, nb, chain_ref, hot_ref, tok_ref, cemb_ref, hemb_ref, w_ref, bias_ref, wout_ref, out_ref,
-    x_all, table, cond, w_t, kv, q_all, gate_all, gout, gin, wo,
+    x_all, table, cond, w_v, w_t, bias_v, bias_f, sc, kv, q_all, gate_all, gout, gin, wo, local_sem,
     xs_sem, xr_sem, ws_sem, wr_sem, ks_sem, kr_sem, gs_sem, gr_sem,
 ):
     samples, td, width = tok_ref.shape
@@ -41,6 +42,9 @@
     b = lax.axis_index("blk")
     bits = [1 << k for k in range(nb.bit_length() - 1)]
 
+    w_copy = pltpu.make_async_copy(w_ref, w_v, local_sem.at[0])
+    wo_copy = pltpu.make_async_copy(wout_ref, wo.at[z], local_sem.at[1])
+    bias_copy = pltpu.make_async_copy(bias_ref, bias_v, local_sem.at[2])
     barrier = pltpu.get_barrier_semaphore()
     for o in range(1, n):
         pl.semaphore_signal(
@@ -50,6 +54,10 @@
         pl.semaphore_signal(
             barrier, inc=1, device_id={"blk": flip(b, bit, nb), "head": z}, device_id_type=MESH
         )
+
+    w_copy.start()
+    bias_copy.start()
+    wo_copy.start()
 
     def line_copy(at, send, recv, block, to):
         return pltpu.make_async_remote_copy(
@@ -146,7 +154,7 @@
     picks = jnp.where(lanes == chain, 1.0, jnp.where(lanes == chains, hot.astype(jnp.float32), 0.0))
     table[...] = jnp.zeros_like(table)
     table[0:chains] = cemb_ref[...].astype(jnp.float32)
-    table[chains : chains + 1] = hemb_ref[...].astype(jnp.float32)
+    table[chains : chains + 1] = hemb_ref[...].astype(jnp.float32).reshape(1, width)
     cond[...] = jnp.dot(
         picks.astype(jnp.bfloat16), table[...].astype(jnp.bfloat16), preferred_element_type=jnp.float32
     )
@@ -164,15 +172,18 @@
 
     lax.fori_loop(0, samples, normalize, 0)
 
-    wo[z] = wout_ref[...]
+    w_copy.wait()
     tile = 128 if w_ref.shape[1] % 128 == 0 else w_ref.shape[1]
     for c in range(0, w_ref.shape[1], tile):
-        w_t[c : c + tile] = w_ref[:, c : c + tile].astype(jnp.float32).T.astype(jnp.bfloat16)
+        w_t[c : c + tile] = w_v[:, c : c + tile].astype(jnp.float32).T.astype(jnp.bfloat16)
 
     evens = [r for r in range(2, nb, 2)]
     levels = max(bin(r).count("1") for r in evens)
     attend_lag = levels + 1
     out_lag = attend_lag + 1
+
+    per = 2
+    chunks = nb // per
 
     def at_sample(s, act):
         @pl.when((s >= 0) & (s < samples))
@@ -194,7 +205,7 @@
             kv_send(s, bit).start()
         for h in range(hh):
             base = h * 4 * HD
-            q_all[s, h] = (proj[base : base + HD] * (1.0 / HD**0.5)).T.astype(jnp.bfloat16)
+            q_all[s, h] = (proj[base : base + HD] * (LOG2E / HD**0.5)).T.astype(jnp.bfloat16)
             gate_all[s, h] = jax.nn.sigmoid(proj[base + 3 * HD : base + 4 * HD]).T
 
     def forward(level):
@@ -226,21 +237,41 @@
     def attend(s):
         for r in range(1, nb, 2):
             kv_recv(s, r)
-        ones = jnp.ones((16, nb * tb), jnp.bfloat16)
-        parts = []
-        for h in range(hh):
-            key = jnp.concatenate([kv[s, a, h * HD : (h + 1) * HD, :] for a in range(nb)], axis=1)
-            value = jnp.concatenate(
-                [kv[s, a, cols + h * HD : cols + (h + 1) * HD, :] for a in range(nb)], axis=1
-            )
-            scores = jnp.dot(q_all[s, h], key, preferred_element_type=jnp.float32)
-            scores = scores + bias_ref[h].astype(jnp.float32)
-            top = jnp.max(scores, axis=-1, keepdims=True)
-            probs = jnp.exp(scores - top).astype(jnp.bfloat16)
-            weighted = lax.dot_general(
-                probs, jnp.concatenate([value, ones], axis=0), (((1,), (1,)), ((), ())),
+        ones = jnp.ones((16, per * tb), jnp.bfloat16)
+
+        def chunk(h, c, first):
+            base = first + h * HD
+            blocks = [kv[s, a, base : base + HD, :] for a in range(c * per, (c + 1) * per)]
+            return jnp.concatenate(blocks, axis=1)
+
+        def score(h, c):
+            here = slice(c * per * tb, (c + 1) * per * tb)
+            part = jnp.dot(q_all[s, h], chunk(h, c, 0), preferred_element_type=jnp.float32)
+            part = part + bias_f[h, :, here]
+            sc[h % 2, :, here] = part
+            top = part[:, :tb]
+            for i in range(1, per):
+                top = jnp.maximum(top, part[:, i * tb : (i + 1) * tb])
+            return top
+
+        def weigh(h, c, top):
+            here = slice(c * per * tb, (c + 1) * per * tb)
+            probs = jnp.exp2((sc[h % 2, :, here] - top).astype(jnp.bfloat16))
+            return lax.dot_general(
+                probs, jnp.concatenate([chunk(h, c, cols), ones], axis=0), (((1,), (1,)), ((), ())),
                 preferred_element_type=jnp.float32,
             )
+
+        parts = []
+        tops = [score(0, c) for c in range(chunks)]
+        for h in range(hh):
+            top = jnp.max(functools.reduce(jnp.maximum, tops), axis=-1, keepdims=True)
+            tops, weighted = [], None
+            for c in range(chunks):
+                if h + 1 < hh:
+                    tops.append(score(h + 1, c))
+                part = weigh(h, c, top)
+                weighted = part if weighted is None else weighted + part
             parts.append(weighted[:, :HD] / weighted[:, HD : HD + 1] * gate_all[s, h])
         gated = jnp.concatenate(parts, axis=1)
         for j in range(n):
@@ -252,10 +283,14 @@
     def project_out(s):
         for o in range(1, n):
             gated_recv(s, o)
-        total = jnp.zeros((td, width), jnp.float32)
-        for j in range(n):
-            total = total + jnp.dot(gin[s, j], wo[j], preferred_element_type=jnp.float32)
-        out_ref[s] = total.astype(out_ref.dtype)
+
+        @pl.when(s % 2 == 1)
+        def _():
+            total = jnp.zeros((2 * td, width), jnp.float32)
+            for j in range(n):
+                pair = gin[pl.ds(s - 1, 2), j].reshape(2 * td, cols)
+                total = total + jnp.dot(pair, wo[j], preferred_element_type=jnp.float32)
+            out_ref[pl.ds(s - 1, 2)] = total.reshape(2, td, width).astype(out_ref.dtype)
 
     def step(t, carry):
         for d in range(1, n):
@@ -270,13 +305,17 @@
             at_sample(t - level, forward(level))
         at_sample(t, project)
 
-        @pl.when(t == 0)
-        def _():
+        @pl.when(t == 1)
+        def _():
+            wo_copy.wait()
+            bias_copy.wait()
+            for h in range(hh):
+                bias_f[h] = bias_v[h].astype(jnp.float32) * LOG2E
             line_send(*w_line, 1, lambda copy: copy.start())
 
         for d in range(1, n):
 
-            @pl.when(t == min(d + 1, out_lag))
+            @pl.when(t == min(d + 2, out_lag + 1))
             def _(d=d):
                 line_recv(*w_line, d)
                 if d + 1 < n:
@@ -313,19 +352,24 @@
     return pl.pallas_call(
         functools.partial(kernel, n, nb),
         out_shape=jax.ShapeDtypeStruct((samples, td, width), bf16),
-        in_specs=[smem, smem] + [vmem] * 6,
+        in_specs=[smem, smem] + [vmem] * 3 + [pl.BlockSpec(memory_space=pl.ANY)] * 3,
         out_specs=vmem,
         scratch_shapes=[
             pltpu.VMEM((samples, n, td, width), bf16),
             pltpu.VMEM((128, width), f32),
             pltpu.VMEM((td, width), f32),
+            pltpu.VMEM(w_proj.shape, bf16),
             pltpu.VMEM((w_proj.shape[1], width), bf16),
+            pltpu.VMEM(pair_bias.shape, bf16),
+            pltpu.VMEM(pair_bias.shape, f32),
+            pltpu.VMEM((2, tb, keys), f32),
             pltpu.VMEM((samples, nb, 2 * cols, tb), bf16),
             pltpu.VMEM((samples, hh, tb, HD), bf16),
             pltpu.VMEM((samples, hh, tb, HD), f32),
             pltpu.VMEM((samples, n, td, cols), bf16),
             pltpu.VMEM((samples, n, td, cols), bf16),
             pltpu.VMEM((n, cols, width), bf16),
+            dma((3,)),
             dma((samples, 2, n - 1)),
             dma((samples, 2, n - 1)),
             dma((2, n - 1)),
@@ -338,7 +382,7 @@
         compiler_params=pltpu.CompilerParams(
             collective_id=0, has_side_effects=True, vmem_limit_bytes=56 * 1024 * 1024
         ),
-    )(chain_id, hotspots, tokens, chain_embed, hot_embed.reshape(1, width), w_proj, pair_bias, w_out)
+    )(chain_id, hotspots, tokens, chain_embed, hot_embed, w_proj, pair_bias, w_out)
 
 
 def solution(mesh):

time: 87.1 us -> 81.9 us (0.940)
  Pallas kernels: 83.8 us -> 79.9 us
  local copies, waits for them, and re-layouts: 3.03 us -> 1.77 us
    pallas_call x1, Pallas kernels: 83.8 us -> 79.9 us  [body(): pl.pallas_call(functools.partial(kernel, n, nb), out_shape=jax.ShapeDtype...]
    reshape x1 -> x0, local copies, waits for them, and re-layouts: 1.26 us -> none  [body(): hot_embed.reshape(1, width)]
where the time goes in v2:
time: 81.9 us; the launch traced here: 81.7 us
  Pallas kernels  79.9 us (98%)
  local copies, waits for them, and re-layouts  1.77 us (2%)
    pallas_call x1, Pallas kernels, body(): pl.pallas_call(functools.partial(kernel, n, nb), out_shape=jax.ShapeDtype...  79.9 us
    unnamed x1, local copies, waits for them, and re-layouts  1.77 us

profile of v2, /device:TPU:0, one launch (start us, length us, event | category | flops | bytes accessed | tf_op | source)
XLA Modules:
  0.0 81.7 jit_solution(11665344507950887144)
XLA Ops:
  0.0 79.9 %shard_map.82 = bf16[8,32,768]{2,1,0:T(8,128)(2,1)} custom-call(s32[32]{0:T(128)} %chain_ref.1, s32[16]{0:T(128)} %hot_ref.1, bf16[8,32,768]{2,1,0:T(8,128)(2,1)} %tok_ref.1, bf16[4,768]{1,0:T(4,128)(2,1)} %cemb_ref.1, bf16[768]{0:T(1024)(128)(2,1)} %hemb_ref.1, bf16[768,768]{1,0:T(8,128)(2,1)} %w_ref.1, bf16[4,128,1024]{2,1,0:T(8,128)(2,1)} %bias_ref.1, ...), custom_call_target="tpu_custom_call" | custom-call | tf_op jit(solution)/shard_map/pallas_call | solution.py:352
  79.9 1.8 %copy.10 = bf16[8,32,768]{2,1,0:T(8,128)(2,1)} copy(bf16[8,32,768]{2,1,0:T(8,128)(2,1)} %shard_map.82) | data formatting | bytes 786432

commit v3 on v2

--- a/solution.py
+++ b/solution.py
@@ -30,9 +30,9 @@
 
 
 def kernel(
-    n, nb, chain_ref, hot_ref, tok_ref, cemb_ref, hemb_ref, w_ref, bias_ref, wout_ref, out_ref,
-    x_all, table, cond, w_v, w_t, bias_v, bias_f, sc, kv, q_all, gate_all, gout, gin, wo, local_sem,
-    xs_sem, xr_sem, ws_sem, wr_sem, ks_sem, kr_sem, gs_sem, gr_sem,
+    n, nb, chain_ref, hot_ref, tok_ref, cemb_ref, hemb_ref, w_ref, bias_ref, out_ref,
+    x_all, table, cond, w_v, w_t, bias_v, bias_f, sc, kv, q_all, gate_all, gout, gin, local_sem,
+    xs_sem, xr_sem, ks_sem, kr_sem, gs_sem, gr_sem,
 ):
     samples, td, width = tok_ref.shape
     hh = bias_ref.shape[0]
@@ -43,8 +43,7 @@
     bits = [1 << k for k in range(nb.bit_length() - 1)]
 
     w_copy = pltpu.make_async_copy(w_ref, w_v, local_sem.at[0])
-    wo_copy = pltpu.make_async_copy(wout_ref, wo.at[z], local_sem.at[1])
-    bias_copy = pltpu.make_async_copy(bias_ref, bias_v, local_sem.at[2])
+    bias_copy = pltpu.make_async_copy(bias_ref, bias_v, local_sem.at[1])
     barrier = pltpu.get_barrier_semaphore()
     for o in range(1, n):
         pl.semaphore_signal(
@@ -57,7 +56,6 @@
 
     w_copy.start()
     bias_copy.start()
-    wo_copy.start()
 
     def line_copy(at, send, recv, block, to):
         return pltpu.make_async_remote_copy(
@@ -89,12 +87,6 @@
             lambda way, d: xs_sem.at[s, way, d - 1],
             lambda way, d: xr_sem.at[s, way, d - 1],
         )
-
-    w_line = (
-        lambda j: wo.at[j],
-        lambda way, d: ws_sem.at[way, d - 1],
-        lambda way, d: wr_sem.at[way, d - 1],
-    )
 
     def route(s, r):
         if r % 2:
@@ -179,7 +171,8 @@
 
     evens = [r for r in range(2, nb, 2)]
     levels = max(bin(r).count("1") for r in evens)
-    attend_lag = levels + 1
+    slack = 2
+    attend_lag = slack * levels + 1
     out_lag = attend_lag + 1
 
     per = 2
@@ -280,19 +273,15 @@
             gated_copy(s, o).start()
         gin[s, z] = gout[s, z]
 
-    def project_out(s):
+    def collect(s):
         for o in range(1, n):
             gated_recv(s, o)
-
-        @pl.when(s % 2 == 1)
-        def _():
-            total = jnp.zeros((2 * td, width), jnp.float32)
-            for j in range(n):
-                pair = gin[pl.ds(s - 1, 2), j].reshape(2 * td, cols)
-                total = total + jnp.dot(pair, wo[j], preferred_element_type=jnp.float32)
-            out_ref[pl.ds(s - 1, 2)] = total.reshape(2, td, width).astype(out_ref.dtype)
-
-    def step(t, carry):
+        out_ref[s] = gin[s]
+
+    ahead = slack * (n - 2)
+
+    def step(i, carry):
+        t = i - ahead
         for d in range(1, n):
 
             def hop(s, d=d):
@@ -300,32 +289,22 @@
                 if d + 1 < n:
                     line_send(*x_line(s), d + 1, lambda copy: copy.start())
 
-            at_sample(t + (n - 1 - d), hop)
+            at_sample(t + slack * (n - 1 - d), hop)
         for level in range(1, levels + 1):
-            at_sample(t - level, forward(level))
+            at_sample(t - slack * level, forward(level))
         at_sample(t, project)
 
-        @pl.when(t == 1)
-        def _():
-            wo_copy.wait()
+        @pl.when(t == 0)
+        def _():
             bias_copy.wait()
             for h in range(hh):
                 bias_f[h] = bias_v[h].astype(jnp.float32) * LOG2E
-            line_send(*w_line, 1, lambda copy: copy.start())
-
-        for d in range(1, n):
-
-            @pl.when(t == min(d + 2, out_lag + 1))
-            def _(d=d):
-                line_recv(*w_line, d)
-                if d + 1 < n:
-                    line_send(*w_line, d + 1, lambda copy: copy.start())
 
         at_sample(t - attend_lag, attend)
-        at_sample(t - out_lag, project_out)
+        at_sample(t - out_lag, collect)
         return carry
 
-    lax.fori_loop(-(n - 2), samples + out_lag, step, 0)
+    lax.fori_loop(0, ahead + samples + out_lag, step, 0)
 
     def drain(s, carry):
         for d in range(1, n):
@@ -337,8 +316,18 @@
         return carry
 
     lax.fori_loop(0, samples, drain, 0)
-    for d in range(1, n):
-        line_send(*w_line, d, lambda copy: copy.wait_send())
+
+
+def out_kernel(gated_ref, w_ref, out_ref):
+    samples, n, td, cols = gated_ref.shape
+    width = w_ref.shape[1]
+    total = jnp.zeros((samples * td, width), jnp.float32)
+    for j in range(n):
+        share = gated_ref[:, j].reshape(samples * td, cols)
+        total = total + jnp.dot(
+            share, w_ref[j * cols : (j + 1) * cols], preferred_element_type=jnp.float32
+        )
+    out_ref[...] = total.reshape(samples, td, width).astype(out_ref.dtype)
 
 
 def body(n, nb, tokens, chain_id, hotspots, chain_embed, hot_embed, w_proj, pair_bias, w_out):
@@ -349,10 +338,11 @@
     vmem = pl.BlockSpec(memory_space=pltpu.VMEM)
     bf16, f32 = jnp.bfloat16, jnp.float32
     dma = pltpu.SemaphoreType.DMA
-    return pl.pallas_call(
+    w_all = lax.all_gather(w_out, "head", axis=0, tiled=True)
+    gated = pl.pallas_call(
         functools.partial(kernel, n, nb),
-        out_shape=jax.ShapeDtypeStruct((samples, td, width), bf16),
-        in_specs=[smem, smem] + [vmem] * 3 + [pl.BlockSpec(memory_space=pl.ANY)] * 3,
+        out_shape=jax.ShapeDtypeStruct((samples, n, td, cols), bf16),
+        in_specs=[smem, smem] + [vmem] * 3 + [pl.BlockSpec(memory_space=pl.ANY)] * 2,
         out_specs=vmem,
         scratch_shapes=[
             pltpu.VMEM((samples, n, td, width), bf16),
@@ -368,12 +358,9 @@
             pltpu.VMEM((samples, hh, tb, HD), f32),
             pltpu.VMEM((samples, n, td, cols), bf16),
             pltpu.VMEM((samples, n, td, cols), bf16),
-            pltpu.VMEM((n, cols, width), bf16),
-            dma((3,)),
+            dma((2,)),
             dma((samples, 2, n - 1)),
             dma((samples, 2, n - 1)),
-            dma((2, n - 1)),
-            dma((2, n - 1)),
             dma((samples, nb)),
             dma((samples, nb)),
             dma((samples, n)),
@@ -382,7 +369,14 @@
         compiler_params=pltpu.CompilerParams(
             collective_id=0, has_side_effects=True, vmem_limit_bytes=56 * 1024 * 1024
         ),
-    )(chain_id, hotspots, tokens, chain_embed, hot_embed, w_proj, pair_bias, w_out)
+    )(chain_id, hotspots, tokens, chain_embed, hot_embed, w_proj, pair_bias)
+    return pl.pallas_call(
+        out_kernel,
+        out_shape=jax.ShapeDtypeStruct((samples, td, width), bf16),
+        in_specs=[vmem, vmem],
+        out_specs=vmem,
+        compiler_params=pltpu.CompilerParams(vmem_limit_bytes=32 * 1024 * 1024),
+    )(gated, w_all)
 
 
 def solution(mesh):

time: 81.9 us -> 99.6 us (1.22)
  between operations: 0.01 us -> 13.4 us
  Pallas kernels: 79.9 us -> 83 us
    pallas_call x1, Pallas kernels: 79.9 us -> 81.6 us  [body(): pl.pallas_call(functools.partial(kernel, n, nb), out_shape=jax.ShapeDtype...]
    pallas_call x0 -> x1, Pallas kernels: none -> 1.31 us  [body(): pl.pallas_call(out_kernel, out_shape=jax.ShapeDtypeStruct((samples, td, w...]
    unnamed x1 -> x4, local copies, waits for them, and re-layouts: 1.77 us -> 2.3 us
  transfers between devices with their start and end apart: 0 -> 1, of which waited for: 0 -> 0; matrix products, arithmetic and copies ran while one was open for 0% -> 0% of each run, Pallas kernels for 0% -> 82%
where the time goes in v3:
time: 99.6 us; the launch traced here: 99.4 us
  Pallas kernels  83 us (83%)
  between operations  13.4 us (13%)
  local copies, waits for them, and re-layouts  2.3 us (2%)
    pallas_call x1, Pallas kernels, body(): pl.pallas_call(functools.partial(kernel, n, nb), out_shape=jax.ShapeDtype...  81.6 us
    unnamed x4, local copies, waits for them, and re-layouts  2.3 us
  transfers between devices with their start and end apart: 1, of which 0 were waited for; matrix products, arithmetic and copies ran while one was open for 0% of the time, Pallas kernels for 82%

profile of v3, /device:TPU:0, one launch (start us, length us, event | category | flops | bytes accessed | tf_op | source)
XLA Modules:
  0.0 99.4 jit_solution(12179600462467802531)
XLA Ops:
  6.5 0.0 all-gather.2.cloned.1.call-start
  6.5 0.7 all-gather.2.cloned.1.call-update
  7.3 81.6 %shard_map.82.gated_ref = bf16[8,4,32,192]{3,2,1,0:T(8,128)(2,1)} custom-call(s32[32]{0:T(128)} %chain_ref.1, s32[16]{0:T(128)} %hot_ref.1, bf16[8,32,768]{2,1,0:T(8,128)(2,1)} %tok_ref.1, bf16[4,768]{1,0:T(4,128)(2,1)} %cemb_ref.1, bf16[768]{0:T(1024)(128)(2,1)} %hemb_ref.1, bf16[768,768]{1,0:T(8,128)(2,1)} %w_ref.1, bf16[4,128,1024]{2,1,0:T(8,128)(2,1)} %bias_ref.1), custom_call_target="tpu_custom_call" | custom-call | tf_op jit(solution)/shard_map/pallas_call | solution.py:342
  88.9 0.0 all-gather.2.cloned.1.call-done.w_ref
  88.9 0.0 copy-start
  88.9 1.0 %copy-done = bf16[8,4,32,192]{3,2,1,0:T(8,128)(2,1)S(1)} copy-done((bf16[8,4,32,192]{3,2,1,0:T(8,128)(2,1)S(1)}, bf16[8,4,32,192]{3,2,1,0:T(8,128)(2,1)}, u32[]{:S(2)}) %copy-start) | copy-done | bytes 393240
  90.0 0.0 copy-start.1
  90.0 1.3 %copy-done.1 = bf16[768,768]{1,0:T(8,128)(2,1)S(1)} copy-done((bf16[768,768]{1,0:T(8,128)(2,1)S(1)}, bf16[768,768]{1,0:T(8,128)(2,1)}, u32[]{:S(2)}) %copy-start.1) | copy-done | bytes 1179672
  91.2 1.3 %shard_map.83 = bf16[8,32,768]{2,1,0:T(8,128)(2,1)} custom-call(bf16[8,4,32,192]{3,2,1,0:T(8,128)(2,1)S(1)} %copy-done, bf16[768,768]{1,0:T(8,128)(2,1)S(1)} %copy-done.1), custom_call_target="tpu_custom_call" | custom-call | tf_op jit(solution)/shard_map/pallas_call | solution.py:373
Async XLA Ops:
  6.5 82.4 %all-gather.2.cloned.1.call-start = ((), (), s32[]{:S(2)}) async-start(), calls=%async_computation | async-start | bytes 1474560 | tf_op jit(solution)/shard_map/all_gather | solution.py:341
  88.9 1.0 %copy-start = (bf16[8,4,32,192]{3,2,1,0:T(8,128)(2,1)S(1)}, bf16[8,4,32,192]{3,2,1,0:T(8,128)(2,1)}, u32[]{:S(2)}) copy-start(bf16[8,4,32,192]{3,2,1,0:T(8,128)(2,1)} %shard_map.82.gated_ref) | copy-start | bytes 1179652
  90.0 1.3 %copy-start.1 = (bf16[768,768]{1,0:T(8,128)(2,1)S(1)}, bf16[768,768]{1,0:T(8,128)(2,1)}, u32[]{:S(2)}) copy-start(bf16[768,768]{1,0:T(8,128)(2,1)} %all-gather.2.cloned.1.call-done.w_ref) | copy-start | bytes 3538948
Sparse Core Ops, SparseCore 0:
  8.9 41.8 all-gather.1

commit v4 on v2

--- a/solution.py
+++ b/solution.py
@@ -11,16 +11,6 @@
 MESH = pl.DeviceIdType.MESH
 
 
-def flip(index, bits, count):
-    total = 0
-    weight = 1
-    while weight < count:
-        bit = (index // weight) % 2
-        total = total + ((1 - bit) if (bits // weight) % 2 else bit) * weight
-        weight *= 2
-    return total
-
-
 def low_bit(r):
     return r & -r
 
@@ -32,7 +22,7 @@
 def kernel(
     n, nb, chain_ref, hot_ref, tok_ref, cemb_ref, hemb_ref, w_ref, bias_ref, wout_ref, out_ref,
     x_all, table, cond, w_v, w_t, bias_v, bias_f, sc, kv, q_all, gate_all, gout, gin, wo, local_sem,
-    xs_sem, xr_sem, ws_sem, wr_sem, ks_sem, kr_sem, gs_sem, gr_sem,
+    xs_sem, xr_sem, ws_sem, wr_sem, ts_sem, tr_sem, ks_sem, kr_sem, gs_sem, gr_sem,
 ):
     samples, td, width = tok_ref.shape
     hh = bias_ref.shape[0]
@@ -41,27 +31,46 @@
     z = lax.axis_index("head")
     b = lax.axis_index("blk")
     bits = [1 << k for k in range(nb.bit_length() - 1)]
+    digits = [lax.rem(lax.div(b, bit), 2) for bit in bits]
+    flipped = [
+        sum(((1 - digit) if r & bit else digit) * bit for digit, bit in zip(digits, bits))
+        for r in range(nb)
+    ]
+    ring = [lax.rem(z + o, n) for o in range(n)]
+    pieces, _, piece_rows, piece_cols = wo.shape[0], *wo.shape[1:]
+    halves = width // piece_cols
+    piece = [lax.rem(flipped[r], pieces) for r in range(pieces)]
 
     w_copy = pltpu.make_async_copy(w_ref, w_v, local_sem.at[0])
-    wo_copy = pltpu.make_async_copy(wout_ref, wo.at[z], local_sem.at[1])
-    bias_copy = pltpu.make_async_copy(bias_ref, bias_v, local_sem.at[2])
+    bias_copy = pltpu.make_async_copy(bias_ref, bias_v, local_sem.at[1])
+    wo_copies = [
+        pltpu.make_async_copy(
+            wout_ref.at[
+                pl.ds(p // halves * piece_rows, piece_rows), pl.ds(p % halves * piece_cols, piece_cols)
+            ],
+            wo.at[p, 0],
+            local_sem.at[2 + p],
+        )
+        for p in range(pieces)
+    ]
     barrier = pltpu.get_barrier_semaphore()
     for o in range(1, n):
         pl.semaphore_signal(
-            barrier, inc=1, device_id={"blk": b, "head": (z + o) % n}, device_id_type=MESH
+            barrier, inc=1, device_id={"blk": b, "head": ring[o]}, device_id_type=MESH
         )
     for bit in bits:
         pl.semaphore_signal(
-            barrier, inc=1, device_id={"blk": flip(b, bit, nb), "head": z}, device_id_type=MESH
+            barrier, inc=1, device_id={"blk": flipped[bit], "head": z}, device_id_type=MESH
         )
 
     w_copy.start()
     bias_copy.start()
-    wo_copy.start()
+    for copy in wo_copies:
+        copy.start()
 
     def line_copy(at, send, recv, block, to):
         return pltpu.make_async_remote_copy(
-            src_ref=at(block), dst_ref=at(block), send_sem=send, recv_sem=recv,
+            src_ref=at(block, z), dst_ref=at(block, to), send_sem=send, recv_sem=recv,
             device_id={"blk": b, "head": to}, device_id_type=MESH,
         )
 
@@ -77,36 +86,45 @@
     def line_recv(at, send, recv, d):
         @pl.when(z - d >= 0)
         def _():
-            line_copy(at, send(0, d), recv(0, d), z - d, z - 1).wait_recv()
+            line_copy(lambda j, _: at(j, z), send(0, d), recv(0, d), z - d, z - 1).wait_recv()
 
         @pl.when(z + d < n)
         def _():
-            line_copy(at, send(1, d), recv(1, d), z + d, z + 1).wait_recv()
+            line_copy(lambda j, _: at(j, z), send(1, d), recv(1, d), z + d, z + 1).wait_recv()
 
     def x_line(s):
         return (
-            lambda j: x_all.at[s, j],
+            lambda j, _: x_all.at[s, j],
             lambda way, d: xs_sem.at[s, way, d - 1],
             lambda way, d: xr_sem.at[s, way, d - 1],
         )
 
     w_line = (
-        lambda j: wo.at[j],
+        lambda j, at: wo.at[piece[0], lax.rem(j - at + n, n)],
         lambda way, d: ws_sem.at[way, d - 1],
         lambda way, d: wr_sem.at[way, d - 1],
     )
 
+    def w_tree(r, back):
+        step = 1 if r % 2 else low_bit(r)
+        held = piece[r if back else r ^ step]
+        ref = wo.at[held, pl.ds(1, n - 1)]
+        return pltpu.make_async_remote_copy(
+            src_ref=ref, dst_ref=ref, send_sem=ts_sem.at[r], recv_sem=tr_sem.at[r],
+            device_id={"blk": flipped[step], "head": z}, device_id_type=MESH,
+        )
+
     def route(s, r):
         if r % 2:
-            return flip(b, r - 1, nb), flip(b, 1, nb), flip(b, r, nb)
+            return flipped[r - 1], flipped[1], flipped[r]
         first, second = low_bit(r), high_bit(r)
-        odd = s % 2
-        blocks = [flip(b, r ^ step, nb) for step in (second, first)]
-        peers = [flip(b, step, nb) for step in (second, first)]
+        odd = lax.rem(s, 2)
+        blocks = [flipped[r ^ step] for step in (second, first)]
+        peers = [flipped[step] for step in (second, first)]
         return (
             blocks[0] * (1 - odd) + blocks[1] * odd,
             peers[0] * (1 - odd) + peers[1] * odd,
-            flip(b, r, nb),
+            flipped[r],
         )
 
     def kv_send(s, r):
@@ -126,7 +144,7 @@
         ).wait_recv()
 
     def gated_copy(s, o):
-        to = (z + o) % n
+        to = ring[o]
         return pltpu.make_async_remote_copy(
             src_ref=gout.at[s, to], dst_ref=gin.at[s, z],
             send_sem=gs_sem.at[s, o], recv_sem=gr_sem.at[s, o],
@@ -134,7 +152,7 @@
         )
 
     def gated_recv(s, o):
-        source = (z + n - o) % n
+        source = ring[n - o]
         pltpu.make_async_remote_copy(
             src_ref=gin.at[s, source], dst_ref=gin.at[s, source],
             send_sem=gs_sem.at[s, o], recv_sem=gr_sem.at[s, o],
@@ -179,7 +197,8 @@
 
     evens = [r for r in range(2, nb, 2)]
     levels = max(bin(r).count("1") for r in evens)
-    attend_lag = levels + 1
+    slack = 2
+    attend_lag = slack * levels + 1
     out_lag = attend_lag + 1
 
     per = 2
@@ -280,19 +299,46 @@
             gated_copy(s, o).start()
         gin[s, z] = gout[s, z]
 
-    def project_out(s):
+    def w_forward(level):
+        for r in range(2, pieces, 2):
+            if bin(r).count("1") != level:
+                continue
+            w_tree(r, True).wait_recv()
+            w_tree(r + 1, False).start()
+            for bit in bits[1:]:
+                if not r & bit and (r | bit) < pieces and low_bit(r | bit) == bit:
+                    w_tree(r | bit, False).start()
+
+    batch = 4 if samples % 4 == 0 else 1
+
+    def collect(s):
         for o in range(1, n):
             gated_recv(s, o)
 
-        @pl.when(s % 2 == 1)
-        def _():
-            total = jnp.zeros((2 * td, width), jnp.float32)
+        @pl.when(s == batch - 1)
+        def _():
+            for r in range(1, pieces, 2):
+                w_tree(r, True).wait_recv()
+
+        @pl.when(lax.rem(s, batch) == batch - 1)
+        def _():
+            here = pl.ds(s - (batch - 1), batch)
+            total = [jnp.zeros((batch * td, piece_cols), jnp.float32) for _ in range(halves)]
             for j in range(n):
-                pair = gin[pl.ds(s - 1, 2), j].reshape(2 * td, cols)
-                total = total + jnp.dot(pair, wo[j], preferred_element_type=jnp.float32)
-            out_ref[pl.ds(s - 1, 2)] = total.reshape(2, td, width).astype(out_ref.dtype)
-
-    def step(t, carry):
+                share = gin[here, ring[j]].reshape(batch * td, cols)
+                for half in range(halves):
+                    rows = [wo[p, j] for p in range(half, pieces, halves)]
+                    total[half] = total[half] + jnp.dot(
+                        share, jnp.concatenate(rows, axis=0), preferred_element_type=jnp.float32
+                    )
+            for half in range(halves):
+                part = total[half].reshape(batch, td, piece_cols).astype(out_ref.dtype)
+                out_ref[here, :, half * piece_cols : (half + 1) * piece_cols] = part
+
+    ahead = slack * (n - 2)
+
+    def step(i, carry):
+        t = i - ahead
         for d in range(1, n):
 
             def hop(s, d=d):
@@ -300,32 +346,43 @@
                 if d + 1 < n:
                     line_send(*x_line(s), d + 1, lambda copy: copy.start())
 
-            at_sample(t + (n - 1 - d), hop)
+            at_sample(t + slack * (n - 1 - d), hop)
         for level in range(1, levels + 1):
-            at_sample(t - level, forward(level))
+            at_sample(t - slack * level, forward(level))
         at_sample(t, project)
 
-        @pl.when(t == 1)
-        def _():
-            wo_copy.wait()
+        @pl.when(t == 0)
+        def _():
             bias_copy.wait()
             for h in range(hh):
                 bias_f[h] = bias_v[h].astype(jnp.float32) * LOG2E
+            for copy in wo_copies:
+                copy.wait()
             line_send(*w_line, 1, lambda copy: copy.start())
 
         for d in range(1, n):
 
-            @pl.when(t == min(d + 2, out_lag + 1))
+            @pl.when(t == min(d, 3))
             def _(d=d):
                 line_recv(*w_line, d)
                 if d + 1 < n:
                     line_send(*w_line, d + 1, lambda copy: copy.start())
+                else:
+                    for bit in bits:
+                        if bit < pieces:
+                            w_tree(bit, False).start()
+
+        for level in range(1, pieces.bit_length() - 1):
+
+            @pl.when(t == min(n - 1, 3) + 2 * level)
+            def _(level=level):
+                w_forward(level)
 
         at_sample(t - attend_lag, attend)
-        at_sample(t - out_lag, project_out)
+        at_sample(t - out_lag, collect)
         return carry
 
-    lax.fori_loop(-(n - 2), samples + out_lag, step, 0)
+    lax.fori_loop(0, ahead + samples + out_lag, step, 0)
 
     def drain(s, carry):
         for d in range(1, n):
@@ -339,6 +396,8 @@
     lax.fori_loop(0, samples, drain, 0)
     for d in range(1, n):
         line_send(*w_line, d, lambda copy: copy.wait_send())
+    for r in range(1, pieces):
+        w_tree(r, False).wait_send()
 
 
 def body(n, nb, tokens, chain_id, hotspots, chain_embed, hot_embed, w_proj, pair_bias, w_out):
@@ -349,6 +408,7 @@
     vmem = pl.BlockSpec(memory_space=pltpu.VMEM)
     bf16, f32 = jnp.bfloat16, jnp.float32
     dma = pltpu.SemaphoreType.DMA
+    pieces, piece_cols = 2 * hh, width // 2
     return pl.pallas_call(
         functools.partial(kernel, n, nb),
         out_shape=jax.ShapeDtypeStruct((samples, td, width), bf16),
@@ -368,12 +428,14 @@
             pltpu.VMEM((samples, hh, tb, HD), f32),
             pltpu.VMEM((samples, n, td, cols), bf16),
             pltpu.VMEM((samples, n, td, cols), bf16),
-            pltpu.VMEM((n, cols, width), bf16),
-            dma((3,)),
+            pltpu.VMEM((pieces, n, HD, piece_cols), bf16),
+            dma((2 + pieces,)),
             dma((samples, 2, n - 1)),
             dma((samples, 2, n - 1)),
             dma((2, n - 1)),
             dma((2, n - 1)),
+            dma((pieces,)),
+            dma((pieces,)),
             dma((samples, nb)),
             dma((samples, nb)),
             dma((samples, n)),

time: 81.9 us -> 71 us (0.87)
  Pallas kernels: 79.9 us -> 69.1 us
    pallas_call x1, Pallas kernels: 79.9 us -> 69.1 us  [body(): pl.pallas_call(functools.partial(kernel, n, nb), out_shape=jax.ShapeDtype...]
where the time goes in v4:
time: 71 us; the launch traced here: 70.9 us
  Pallas kernels  69.1 us (97%)
  local copies, waits for them, and re-layouts  1.77 us (2%)
    pallas_call x1, Pallas kernels, body(): pl.pallas_call(functools.partial(kernel, n, nb), out_shape=jax.ShapeDtype...  69.1 us
    unnamed x1, local copies, waits for them, and re-layouts  1.77 us

profile of v4, /device:TPU:0, one launch (start us, length us, event | category | flops | bytes accessed | tf_op | source)
XLA Modules:
  0.0 70.9 jit_solution(11789448367146979758)
XLA Ops:
  0.0 69.1 %shard_map.82 = bf16[8,32,768]{2,1,0:T(8,128)(2,1)} custom-call(s32[32]{0:T(128)} %chain_ref.1, s32[16]{0:T(128)} %hot_ref.1, bf16[8,32,768]{2,1,0:T(8,128)(2,1)} %tok_ref.1, bf16[4,768]{1,0:T(4,128)(2,1)} %cemb_ref.1, bf16[768]{0:T(1024)(128)(2,1)} %hemb_ref.1, bf16[768,768]{1,0:T(8,128)(2,1)} %w_ref.1, bf16[4,128,1024]{2,1,0:T(8,128)(2,1)} %bias_ref.1, ...), custom_call_target="tpu_custom_call" | custom-call | tf_op jit(solution)/shard_map/pallas_call | solution.py:412
  69.1 1.8 %copy.10 = bf16[8,32,768]{2,1,0:T(8,128)(2,1)} copy(bf16[8,32,768]{2,1,0:T(8,128)(2,1)} %shard_map.82) | data formatting | bytes 786432

commit v5 on v4

--- a/solution.py
+++ b/solution.py
@@ -185,8 +185,14 @@
         centered = shifted - average
         spread = jnp.mean(centered * centered, axis=-1, keepdims=True)
         x_all[s, z] = (centered * lax.rsqrt(spread + 1e-05)).astype(jnp.bfloat16)
-        line_send(*x_line(s), 1, lambda copy: copy.start())
+
+        @pl.when(s < early)
+        def _():
+            line_send(*x_line(s), 1, lambda copy: copy.start())
+
         return carry
+
+    early = 2
 
     lax.fori_loop(0, samples, normalize, 0)
 
@@ -197,8 +203,7 @@
 
     evens = [r for r in range(2, nb, 2)]
     levels = max(bin(r).count("1") for r in evens)
-    slack = 2
-    attend_lag = slack * levels + 1
+    attend_lag = levels + 1
     out_lag = attend_lag + 1
 
     per = 2
@@ -335,7 +340,7 @@
                 part = total[half].reshape(batch, td, piece_cols).astype(out_ref.dtype)
                 out_ref[here, :, half * piece_cols : (half + 1) * piece_cols] = part
 
-    ahead = slack * (n - 2)
+    ahead = n - 2
 
     def step(i, carry):
         t = i - ahead
@@ -346,12 +351,13 @@
                 if d + 1 < n:
                     line_send(*x_line(s), d + 1, lambda copy: copy.start())
 
-            at_sample(t + slack * (n - 1 - d), hop)
+            at_sample(t + (n - 1 - d), hop)
+        at_sample(t + ahead + early, lambda s: line_send(*x_line(s), 1, lambda copy: copy.start()))
+        at_sample(t, project)
         for level in range(1, levels + 1):
-            at_sample(t - slack * level, forward(level))
-        at_sample(t, project)
-
-        @pl.when(t == 0)
+            at_sample(t - level, forward(level))
+
+        @pl.when(t == -1)
         def _():
             bias_copy.wait()
             for h in range(hh):
@@ -362,7 +368,7 @@
 
         for d in range(1, n):
 
-            @pl.when(t == min(d, 3))
+            @pl.when(t == min(d, 3) - 1)
             def _(d=d):
                 line_recv(*w_line, d)
                 if d + 1 < n:
@@ -374,7 +380,7 @@
 
         for level in range(1, pieces.bit_length() - 1):
 
-            @pl.when(t == min(n - 1, 3) + 2 * level)
+            @pl.when(t == min(n - 1, 3) - 1 + 2 * level)
             def _(level=level):
                 w_forward(level)
 

time: 71 us -> 66.5 us (0.937)
  Pallas kernels: 69.1 us -> 64.6 us
    pallas_call x1, Pallas kernels: 69.1 us -> 64.6 us  [body(): pl.pallas_call(functools.partial(kernel, n, nb), out_shape=jax.ShapeDtype...]
where the time goes in v5:
time: 66.5 us; the launch traced here: 66.3 us
  Pallas kernels  64.6 us (97%)
  local copies, waits for them, and re-layouts  1.77 us (3%)
    pallas_call x1, Pallas kernels, body(): pl.pallas_call(functools.partial(kernel, n, nb), out_shape=jax.ShapeDtype...  64.6 us
    unnamed x1, local copies, waits for them, and re-layouts  1.77 us

profile of v5, /device:TPU:0, one launch (start us, length us, event | category | flops | bytes accessed | tf_op | source)
XLA Modules:
  0.0 66.3 jit_solution(18219622965894396379)
XLA Ops:
  0.0 64.6 %shard_map.82 = bf16[8,32,768]{2,1,0:T(8,128)(2,1)} custom-call(s32[32]{0:T(128)} %chain_ref.1, s32[16]{0:T(128)} %hot_ref.1, bf16[8,32,768]{2,1,0:T(8,128)(2,1)} %tok_ref.1, bf16[4,768]{1,0:T(4,128)(2,1)} %cemb_ref.1, bf16[768]{0:T(1024)(128)(2,1)} %hemb_ref.1, bf16[768,768]{1,0:T(8,128)(2,1)} %w_ref.1, bf16[4,128,1024]{2,1,0:T(8,128)(2,1)} %bias_ref.1, ...), custom_call_target="tpu_custom_call" | custom-call | tf_op jit(solution)/shard_map/pallas_call | solution.py:418
  64.6 1.8 %copy.10 = bf16[8,32,768]{2,1,0:T(8,128)(2,1)} copy(bf16[8,32,768]{2,1,0:T(8,128)(2,1)} %shard_map.82) | data formatting | bytes 786432

commit v6 on v5

--- a/solution.py
+++ b/solution.py
@@ -131,7 +131,7 @@
         block, peer, _ = route(s, r)
         return pltpu.make_async_remote_copy(
             src_ref=kv.at[s, block], dst_ref=kv.at[s, block],
-            send_sem=ks_sem.at[s, r], recv_sem=kr_sem.at[s, r],
+            send_sem=ks_sem.at[s], recv_sem=kr_sem.at[s, 1 if r % 2 else r],
             device_id={"blk": peer, "head": z}, device_id_type=MESH,
         )
 
@@ -139,7 +139,7 @@
         _, peer, mine = route(s, r)
         pltpu.make_async_remote_copy(
             src_ref=kv.at[s, mine], dst_ref=kv.at[s, mine],
-            send_sem=ks_sem.at[s, r], recv_sem=kr_sem.at[s, r],
+            send_sem=ks_sem.at[s], recv_sem=kr_sem.at[s, 1 if r % 2 else r],
             device_id={"blk": peer, "head": z}, device_id_type=MESH,
         ).wait_recv()
 
@@ -147,17 +147,31 @@
         to = ring[o]
         return pltpu.make_async_remote_copy(
             src_ref=gout.at[s, to], dst_ref=gin.at[s, z],
-            send_sem=gs_sem.at[s, o], recv_sem=gr_sem.at[s, o],
+            send_sem=gs_sem.at[s], recv_sem=gr_sem.at[s],
             device_id={"blk": b, "head": to}, device_id_type=MESH,
         )
 
-    def gated_recv(s, o):
-        source = ring[n - o]
-        pltpu.make_async_remote_copy(
-            src_ref=gin.at[s, source], dst_ref=gin.at[s, source],
-            send_sem=gs_sem.at[s, o], recv_sem=gr_sem.at[s, o],
-            device_id={"blk": b, "head": source}, device_id_type=MESH,
-        ).wait_recv()
+    def whole_copy(ref, send, recv, blk, head):
+        return pltpu.make_async_remote_copy(
+            src_ref=ref, dst_ref=ref, send_sem=send, recv_sem=recv,
+            device_id={"blk": blk, "head": head}, device_id_type=MESH,
+        )
+
+    def sibling_recv(s):
+        ref = kv.at[s, pl.ds(0, nb // 2)]
+        whole_copy(ref, ks_sem.at[s], kr_sem.at[s, 1], flipped[1], z).wait_recv()
+
+    def kv_sent(s):
+        ref = kv.at[s, pl.ds(0, nb - 1)]
+        whole_copy(ref, ks_sem.at[s], kr_sem.at[s, 1], flipped[1], z).wait_send()
+
+    def gated_recv(s):
+        ref = gin.at[s, pl.ds(0, n - 1)]
+        whole_copy(ref, gs_sem.at[s], gr_sem.at[s], b, ring[1]).wait_recv()
+
+    def gated_sent(s):
+        ref = gout.at[s, pl.ds(0, n - 1)]
+        whole_copy(ref, gs_sem.at[s], gr_sem.at[s], b, ring[1]).wait_send()
 
     rows = lax.broadcasted_iota(jnp.int32, (td, 128), 0)
     lanes = lax.broadcasted_iota(jnp.int32, (td, 128), 1)
@@ -179,22 +193,21 @@
 
     pl.semaphore_wait(barrier, n - 1 + len(bits))
 
-    def normalize(s, carry):
+    def normalize(s):
         shifted = tok_ref[s].astype(jnp.float32) + cond[...]
         average = jnp.mean(shifted, axis=-1, keepdims=True)
         centered = shifted - average
         spread = jnp.mean(centered * centered, axis=-1, keepdims=True)
         x_all[s, z] = (centered * lax.rsqrt(spread + 1e-05)).astype(jnp.bfloat16)
-
-        @pl.when(s < early)
-        def _():
-            line_send(*x_line(s), 1, lambda copy: copy.start())
-
-        return carry
-
-    early = 2
-
-    lax.fori_loop(0, samples, normalize, 0)
+        line_send(*x_line(s), 1, lambda copy: copy.start())
+
+    early = min(2, samples)
+    normalize(0)
+    for copy in wo_copies:
+        copy.wait()
+    line_send(*w_line, 1, lambda copy: copy.start())
+    for s in range(1, early):
+        normalize(s)
 
     w_copy.wait()
     tile = 128 if w_ref.shape[1] % 128 == 0 else w_ref.shape[1]
@@ -259,8 +272,7 @@
         return act
 
     def attend(s):
-        for r in range(1, nb, 2):
-            kv_recv(s, r)
+        sibling_recv(s)
         ones = jnp.ones((16, per * tb), jnp.bfloat16)
 
         def chunk(h, c, first):
@@ -317,8 +329,7 @@
     batch = 4 if samples % 4 == 0 else 1
 
     def collect(s):
-        for o in range(1, n):
-            gated_recv(s, o)
+        gated_recv(s)
 
         @pl.when(s == batch - 1)
         def _():
@@ -340,6 +351,12 @@
                 part = total[half].reshape(batch, td, piece_cols).astype(out_ref.dtype)
                 out_ref[here, :, half * piece_cols : (half + 1) * piece_cols] = part
 
+    def drain(s):
+        for d in range(1, n):
+            line_send(*x_line(s), d, lambda copy: copy.wait_send())
+        kv_sent(s)
+        gated_sent(s)
+
     ahead = n - 2
 
     def step(i, carry):
@@ -352,23 +369,10 @@
                     line_send(*x_line(s), d + 1, lambda copy: copy.start())
 
             at_sample(t + (n - 1 - d), hop)
-        at_sample(t + ahead + early, lambda s: line_send(*x_line(s), 1, lambda copy: copy.start()))
-        at_sample(t, project)
-        for level in range(1, levels + 1):
-            at_sample(t - level, forward(level))
-
-        @pl.when(t == -1)
-        def _():
-            bias_copy.wait()
-            for h in range(hh):
-                bias_f[h] = bias_v[h].astype(jnp.float32) * LOG2E
-            for copy in wo_copies:
-                copy.wait()
-            line_send(*w_line, 1, lambda copy: copy.start())
-
+        at_sample(t + ahead + early, normalize)
         for d in range(1, n):
 
-            @pl.when(t == min(d, 3) - 1)
+            @pl.when(t == min(d, ahead + 1) - ahead - 1)
             def _(d=d):
                 line_recv(*w_line, d)
                 if d + 1 < n:
@@ -380,26 +384,27 @@
 
         for level in range(1, pieces.bit_length() - 1):
 
-            @pl.when(t == min(n - 1, 3) - 1 + 2 * level)
+            @pl.when(t == level)
             def _(level=level):
                 w_forward(level)
 
+        at_sample(t, project)
+        for level in range(1, levels + 1):
+            at_sample(t - level, forward(level))
+
+        @pl.when(t == -1)
+        def _():
+            bias_copy.wait()
+            for h in range(hh):
+                bias_f[h] = bias_v[h].astype(jnp.float32) * LOG2E
+
         at_sample(t - attend_lag, attend)
         at_sample(t - out_lag, collect)
+        at_sample(t - out_lag, drain)
         return carry
 
     lax.fori_loop(0, ahead + samples + out_lag, step, 0)
 
-    def drain(s, carry):
-        for d in range(1, n):
-            line_send(*x_line(s), d, lambda copy: copy.wait_send())
-        for r in range(1, nb):
-            kv_send(s, r).wait_send()
-        for o in range(1, n):
-            gated_copy(s, o).wait_send()
-        return carry
-
-    lax.fori_loop(0, samples, drain, 0)
     for d in range(1, n):
         line_send(*w_line, d, lambda copy: copy.wait_send())
     for r in range(1, pieces):
@@ -442,10 +447,10 @@
             dma((2, n - 1)),
             dma((pieces,)),
             dma((pieces,)),
+            dma((samples,)),
             dma((samples, nb)),
-            dma((samples, nb)),
-            dma((samples, n)),
-            dma((samples, n)),
+            dma((samples,)),
+            dma((samples,)),
         ],
         compiler_params=pltpu.CompilerParams(
             collective_id=0, has_side_effects=True, vmem_limit_bytes=56 * 1024 * 1024

time: 66.5 us -> 67 us (level)
  no operation moved by 1% of the time
where the time goes in v6:
time: 67 us; the launch traced here: 66.8 us
  Pallas kernels  65 us (97%)
  local copies, waits for them, and re-layouts  1.77 us (3%)
    pallas_call x1, Pallas kernels, body(): pl.pallas_call(functools.partial(kernel, n, nb), out_shape=jax.ShapeDtype...  65 us
    unnamed x1, local copies, waits for them, and re-layouts  1.77 us

profile of v6, /device:TPU:0, one launch (start us, length us, event | category | flops | bytes accessed | tf_op | source)
XLA Modules:
  0.0 66.8 jit_solution(7871503229292668001)
XLA Ops:
  0.0 65.0 %shard_map.82 = bf16[8,32,768]{2,1,0:T(8,128)(2,1)} custom-call(s32[32]{0:T(128)} %chain_ref.1, s32[16]{0:T(128)} %hot_ref.1, bf16[8,32,768]{2,1,0:T(8,128)(2,1)} %tok_ref.1, bf16[4,768]{1,0:T(4,128)(2,1)} %cemb_ref.1, bf16[768]{0:T(1024)(128)(2,1)} %hemb_ref.1, bf16[768,768]{1,0:T(8,128)(2,1)} %w_ref.1, bf16[4,128,1024]{2,1,0:T(8,128)(2,1)} %bias_ref.1, ...), custom_call_target="tpu_custom_call" | custom-call | tf_op jit(solution)/shard_map/pallas_call | solution.py:423
  65.0 1.8 %copy.10 = bf16[8,32,768]{2,1,0:T(8,128)(2,1)} copy(bf16[8,32,768]{2,1,0:T(8,128)(2,1)} %shard_map.82) | data formatting | bytes 786432

commit v7 on v6

--- a/solution.py
+++ b/solution.py
@@ -389,8 +389,6 @@
                 w_forward(level)
 
         at_sample(t, project)
-        for level in range(1, levels + 1):
-            at_sample(t - level, forward(level))
 
         @pl.when(t == -1)
         def _():
@@ -400,6 +398,8 @@
 
         at_sample(t - attend_lag, attend)
         at_sample(t - out_lag, collect)
+        for level in range(1, levels + 1):
+            at_sample(t - level, forward(level))
         at_sample(t - out_lag, drain)
         return carry
 

time: 67 us -> 66 us (0.985)
  Pallas kernels: 65 us -> 64.1 us
    pallas_call x1, Pallas kernels: 65 us -> 64.1 us  [body(): pl.pallas_call(functools.partial(kernel, n, nb), out_shape=jax.ShapeDtype...]
where the time goes in v7:
time: 66 us; the launch traced here: 65.9 us
  Pallas kernels  64.1 us (97%)
  local copies, waits for them, and re-layouts  1.77 us (3%)
    pallas_call x1, Pallas kernels, body(): pl.pallas_call(functools.partial(kernel, n, nb), out_shape=jax.ShapeDtype...  64.1 us
    unnamed x1, local copies, waits for them, and re-layouts  1.77 us

profile of v7, /device:TPU:0, one launch (start us, length us, event | category | flops | bytes accessed | tf_op | source)
XLA Modules:
  0.0 65.9 jit_solution(3390193009196697723)
XLA Ops:
  0.0 64.1 %shard_map.82 = bf16[8,32,768]{2,1,0:T(8,128)(2,1)} custom-call(s32[32]{0:T(128)} %chain_ref.1, s32[16]{0:T(128)} %hot_ref.1, bf16[8,32,768]{2,1,0:T(8,128)(2,1)} %tok_ref.1, bf16[4,768]{1,0:T(4,128)(2,1)} %cemb_ref.1, bf16[768]{0:T(1024)(128)(2,1)} %hemb_ref.1, bf16[768,768]{1,0:T(8,128)(2,1)} %w_ref.1, bf16[4,128,1024]{2,1,0:T(8,128)(2,1)} %bias_ref.1, ...), custom_call_target="tpu_custom_call" | custom-call | tf_op jit(solution)/shard_map/pallas_call | solution.py:423
  64.1 1.8 %copy.10 = bf16[8,32,768]{2,1,0:T(8,128)(2,1)} copy(bf16[8,32,768]{2,1,0:T(8,128)(2,1)} %shard_map.82) | data formatting | bytes 786432

commit v8 on v7

--- a/solution.py
+++ b/solution.py
@@ -284,7 +284,7 @@
             here = slice(c * per * tb, (c + 1) * per * tb)
             part = jnp.dot(q_all[s, h], chunk(h, c, 0), preferred_element_type=jnp.float32)
             part = part + bias_f[h, :, here]
-            sc[h % 2, :, here] = part
+            sc[h, :, here] = part
             top = part[:, :tb]
             for i in range(1, per):
                 top = jnp.maximum(top, part[:, i * tb : (i + 1) * tb])
@@ -292,22 +292,22 @@
 
         def weigh(h, c, top):
             here = slice(c * per * tb, (c + 1) * per * tb)
-            probs = jnp.exp2((sc[h % 2, :, here] - top).astype(jnp.bfloat16))
+            probs = jnp.exp2((sc[h, :, here] - top).astype(jnp.bfloat16))
             return lax.dot_general(
                 probs, jnp.concatenate([chunk(h, c, cols), ones], axis=0), (((1,), (1,)), ((), ())),
                 preferred_element_type=jnp.float32,
             )
 
         parts = []
-        tops = [score(0, c) for c in range(chunks)]
+        tops = [[score(h, c) for c in range(chunks)] for h in range(hh)]
+        tops = [jnp.max(functools.reduce(jnp.maximum, top), axis=-1, keepdims=True) for top in tops]
+        sums = [None] * hh
+        for c in range(chunks):
+            for h in range(hh):
+                part = weigh(h, c, tops[h])
+                sums[h] = part if sums[h] is None else sums[h] + part
         for h in range(hh):
-            top = jnp.max(functools.reduce(jnp.maximum, tops), axis=-1, keepdims=True)
-            tops, weighted = [], None
-            for c in range(chunks):
-                if h + 1 < hh:
-                    tops.append(score(h + 1, c))
-                part = weigh(h, c, top)
-                weighted = part if weighted is None else weighted + part
+            weighted = sums[h]
             parts.append(weighted[:, :HD] / weighted[:, HD : HD + 1] * gate_all[s, h])
         gated = jnp.concatenate(parts, axis=1)
         for j in range(n):
@@ -433,7 +433,7 @@
             pltpu.VMEM((w_proj.shape[1], width), bf16),
             pltpu.VMEM(pair_bias.shape, bf16),
             pltpu.VMEM(pair_bias.shape, f32),
-            pltpu.VMEM((2, tb, keys), f32),
+            pltpu.VMEM((hh, tb, keys), f32),
             pltpu.VMEM((samples, nb, 2 * cols, tb), bf16),
             pltpu.VMEM((samples, hh, tb, HD), bf16),
             pltpu.VMEM((samples, hh, tb, HD), f32),

time: 66 us -> 65.9 us (level)
  no operation moved by 1% of the time
where the time goes in v8:
time: 65.9 us; the launch traced here: 65.7 us
  Pallas kernels  63.9 us (97%)
  local copies, waits for them, and re-layouts  1.77 us (3%)
    pallas_call x1, Pallas kernels, body(): pl.pallas_call(functools.partial(kernel, n, nb), out_shape=jax.ShapeDtype...  63.9 us
    unnamed x1, local copies, waits for them, and re-layouts  1.77 us

profile of v8, /device:TPU:0, one launch (start us, length us, event | category | flops | bytes accessed | tf_op | source)
XLA Modules:
  0.0 65.7 jit_solution(4469779605364420094)
XLA Ops:
  0.0 63.9 %shard_map.82 = bf16[8,32,768]{2,1,0:T(8,128)(2,1)} custom-call(s32[32]{0:T(128)} %chain_ref.1, s32[16]{0:T(128)} %hot_ref.1, bf16[8,32,768]{2,1,0:T(8,128)(2,1)} %tok_ref.1, bf16[4,768]{1,0:T(4,128)(2,1)} %cemb_ref.1, bf16[768]{0:T(1024)(128)(2,1)} %hemb_ref.1, bf16[768,768]{1,0:T(8,128)(2,1)} %w_ref.1, bf16[4,128,1024]{2,1,0:T(8,128)(2,1)} %bias_ref.1, ...), custom_call_target="tpu_custom_call" | custom-call | tf_op jit(solution)/shard_map/pallas_call | solution.py:423
  64.0 1.8 %copy.10 = bf16[8,32,768]{2,1,0:T(8,128)(2,1)} copy(bf16[8,32,768]{2,1,0:T(8,128)(2,1)} %shard_map.82) | data formatting | bytes 786432

commit v9 on v8

--- a/solution.py
+++ b/solution.py
@@ -237,7 +237,13 @@
             base = h * 4 * HD
             keys.append(proj[base + HD : base + 2 * HD])
             values.append(proj[base + 2 * HD : base + 3 * HD])
-        kv[s, b] = jnp.concatenate(keys + values, axis=0).astype(jnp.bfloat16)
+        ones = jnp.ones((64 - HD, tb), jnp.float32)
+        values = values + [jnp.ones((HD, tb), jnp.float32)] * (hh % 2)
+        pairs = [
+            jnp.concatenate([values[h], ones, values[h + 1], ones], axis=0).T
+            for h in range(0, hh, 2)
+        ]
+        kv[s, b] = jnp.concatenate(keys + pairs, axis=0).astype(jnp.bfloat16)
         for bit in bits:
             kv_send(s, bit).start()
         for h in range(hh):
@@ -273,16 +279,18 @@
 
     def attend(s):
         sibling_recv(s)
-        ones = jnp.ones((16, per * tb), jnp.bfloat16)
-
-        def chunk(h, c, first):
-            base = first + h * HD
-            blocks = [kv[s, a, base : base + HD, :] for a in range(c * per, (c + 1) * per)]
+        def chunk(h, c):
+            blocks = [kv[s, a, h * HD : (h + 1) * HD, :] for a in range(c * per, (c + 1) * per)]
             return jnp.concatenate(blocks, axis=1)
+
+        def value_pair(h, c):
+            base = cols + h // 2 * tb
+            blocks = [kv[s, a, base : base + tb, :] for a in range(c * per, (c + 1) * per)]
+            return jnp.concatenate(blocks, axis=0)
 
         def score(h, c):
             here = slice(c * per * tb, (c + 1) * per * tb)
-            part = jnp.dot(q_all[s, h], chunk(h, c, 0), preferred_element_type=jnp.float32)
+            part = jnp.dot(q_all[s, h], chunk(h, c), preferred_element_type=jnp.float32)
             part = part + bias_f[h, :, here]
             sc[h, :, here] = part
             top = part[:, :tb]
@@ -293,10 +301,7 @@
         def weigh(h, c, top):
             here = slice(c * per * tb, (c + 1) * per * tb)
             probs = jnp.exp2((sc[h, :, here] - top).astype(jnp.bfloat16))
-            return lax.dot_general(
-                probs, jnp.concatenate([chunk(h, c, cols), ones], axis=0), (((1,), (1,)), ((), ())),
-                preferred_element_type=jnp.float32,
-            )
+            return jnp.dot(probs, value_pair(h, c), preferred_element_type=jnp.float32)
 
         parts = []
         tops = [[score(h, c) for c in range(chunks)] for h in range(hh)]
@@ -307,7 +312,7 @@
                 part = weigh(h, c, tops[h])
                 sums[h] = part if sums[h] is None else sums[h] + part
         for h in range(hh):
-            weighted = sums[h]
+            weighted = sums[h][:, h % 2 * 64 : h % 2 * 64 + 64]
             parts.append(weighted[:, :HD] / weighted[:, HD : HD + 1] * gate_all[s, h])
         gated = jnp.concatenate(parts, axis=1)
         for j in range(n):
@@ -434,7 +439,7 @@
             pltpu.VMEM(pair_bias.shape, bf16),
             pltpu.VMEM(pair_bias.shape, f32),
             pltpu.VMEM((hh, tb, keys), f32),
-            pltpu.VMEM((samples, nb, 2 * cols, tb), bf16),
+            pltpu.VMEM((samples, nb, cols + (hh + 1) // 2 * tb, tb), bf16),
             pltpu.VMEM((samples, hh, tb, HD), bf16),
             pltpu.VMEM((samples, hh, tb, HD), f32),
             pltpu.VMEM((samples, n, td, cols), bf16),

time: 65.9 us -> 68.5 us (1.039)
  Pallas kernels: 63.9 us -> 66.5 us
    pallas_call x1, Pallas kernels: 63.9 us -> 66.5 us  [body(): pl.pallas_call(functools.partial(kernel, n, nb), out_shape=jax.ShapeDtype...]
where the time goes in v9:
time: 68.5 us; the launch traced here: 68.3 us
  Pallas kernels  66.5 us (97%)
  local copies, waits for them, and re-layouts  1.77 us (3%)
    pallas_call x1, Pallas kernels, body(): pl.pallas_call(functools.partial(kernel, n, nb), out_shape=jax.ShapeDtype...  66.5 us
    unnamed x1, local copies, waits for them, and re-layouts  1.77 us

profile of v9, /device:TPU:0, one launch (start us, length us, event | category | flops | bytes accessed | tf_op | source)
XLA Modules:
  0.0 68.3 jit_solution(5301415170846298917)
XLA Ops:
  0.0 66.5 %shard_map.82 = bf16[8,32,768]{2,1,0:T(8,128)(2,1)} custom-call(s32[32]{0:T(128)} %chain_ref.1, s32[16]{0:T(128)} %hot_ref.1, bf16[8,32,768]{2,1,0:T(8,128)(2,1)} %tok_ref.1, bf16[4,768]{1,0:T(4,128)(2,1)} %cemb_ref.1, bf16[768]{0:T(1024)(128)(2,1)} %hemb_ref.1, bf16[768,768]{1,0:T(8,128)(2,1)} %w_ref.1, bf16[4,128,1024]{2,1,0:T(8,128)(2,1)} %bias_ref.1, ...), custom_call_target="tpu_custom_call" | custom-call | tf_op jit(solution)/shard_map/pallas_call | solution.py:428
  66.5 1.8 %copy.10 = bf16[8,32,768]{2,1,0:T(8,128)(2,1)} copy(bf16[8,32,768]{2,1,0:T(8,128)(2,1)} %shard_map.82) | data formatting | bytes 786432
